TPU v7x, 1024 devices: a whole 8x8x8 slice. The times are simulated.
1024 devices in a mesh: dp: 32 (over z_hi, y, core), seq: 32 (over z_lo, x).
Axes of the slice: x: 8, y: 8, z: 8 (z_hi: 2, z_lo: 4; z = z_hi * 4 + z_lo), core: 2. Of those that a mesh axis runs over, the one named last changes fastest.
Arguments:
- dna_bases: int32 [32, 32768], P('dp', 'seq'), may hold values from 0 to 4
- conv_weight: bfloat16 [5, 5, 1536], replicated, may hold values from -2.5 to 2.5
- conv_bias: float32 [1536], replicated, may hold values from -3 to 3
- w_query: bfloat16 [1536, 768], replicated, may hold values from -1 to 1
- w_key: bfloat16 [1536, 768], replicated, may hold values from -1 to 1
- w_value: bfloat16 [1536, 768], replicated, may hold values from -0.15625 to 0.15625
- out_grad: bfloat16 [32, 256, 768], P('dp', 'seq'), may hold values from -6 to 6
Outputs:
- attended: bfloat16 [32, 256, 768], P('dp', 'seq')
- pooled: bfloat16 [32, 256, 1536], P('dp', 'seq')
- conv_grad: float32 [5, 5, 1536], replicated
- bias_grad: float32 [1536], replicated
All inputs are finite; a program needn't handle non-finite values.
Results may differ from a plain program's by a relative error of at most 0.0103.
Values may be sent and summed in bfloat16 or wider, within the bound.
A program may use at most 32 MiB of HBM per device.

v0:
```python
import jax
import jax.numpy as jnp
from jax import lax
from jax.sharding import PartitionSpec as P

C = 1536
HEADS = 4
HEAD = 192
KERNEL = 5
LETTERS = 5
POOL = 128
INNER = 768


def padded(block, sides, width):
    for axis, dim in sides:
        count = lax.axis_size(axis)
        forward = [(i, i + 1) for i in range(count - 1)]
        backward = [(target, source) for source, target in forward]
        low = lax.ppermute(
            lax.slice_in_dim(block, block.shape[dim] - width, None, axis=dim), axis, forward
        )
        high = lax.ppermute(lax.slice_in_dim(block, 0, width, axis=dim), axis, backward)
        block = jnp.concatenate([low, block, high], axis=dim)
    return block


def tap_letters(window, tap_count):
    tap_codes = jnp.stack([window[offset : offset + tap_count] for offset in range(KERNEL)], axis=1)
    letter_codes = jnp.arange(1, LETTERS + 1, dtype=jnp.int32)
    return (tap_codes[:, :, None] == letter_codes[None, None, :]).reshape(
        tap_count, KERNEL * LETTERS
    )


def conv_pre(one_hot, conv_weight, conv_bias):
    tap_table = conv_weight.reshape(KERNEL * LETTERS, C)
    return (
        jnp.dot(one_hot.astype(jnp.bfloat16), tap_table, preferred_element_type=jnp.float32)
        + conv_bias
    )


def pooled_rows(extended, conv_weight, conv_bias):
    tap_count = 4 * POOL
    block_count = (extended.shape[1] - 4) // tap_count

    def pooled_one_genome(row_codes):

        def pooled_one_block(block_index):
            window = lax.dynamic_slice_in_dim(row_codes, block_index * tap_count, tap_count + 4)
            activated = jax.nn.gelu(
                conv_pre(tap_letters(window, tap_count), conv_weight, conv_bias)
            )
            return activated.reshape(4, POOL, C).mean(axis=1).astype(jnp.bfloat16)

        blocks_out = lax.map(pooled_one_block, jnp.arange(block_count, dtype=jnp.int32))
        return blocks_out.reshape(block_count * 4, C)

    return lax.map(pooled_one_genome, extended)


def conv_grads(extended, d_pooled, conv_weight, conv_bias):
    tap_count = 4 * POOL
    block_count = (extended.shape[1] - 4) // tap_count
    start_sums = (jnp.zeros((KERNEL * LETTERS, C), jnp.float32), jnp.zeros((C,), jnp.float32))

    def conv_one_genome(totals, pair):
        row_codes, d_rows = pair

        def conv_one_block(sums, block_index):
            window = lax.dynamic_slice_in_dim(row_codes, block_index * tap_count, tap_count + 4)
            one_hot = tap_letters(window, tap_count)
            pre_act = conv_pre(one_hot, conv_weight, conv_bias)
            d_block = lax.dynamic_slice_in_dim(d_rows, block_index * 4, 4, 0)
            d_act = jnp.repeat(d_block, POOL, axis=0) * (1.0 / POOL)
            d_pre = jax.vjp(jax.nn.gelu, pre_act)[1](d_act)[0]
            weight_sum = sums[0] + jnp.einsum(
                "pk,pc->kc", one_hot.astype(jnp.float32), d_pre, precision=lax.Precision.HIGHEST
            )
            return ((weight_sum, sums[1] + jnp.sum(d_pre, axis=0)), None)

        totals, _ = lax.scan(conv_one_block, totals, jnp.arange(block_count, dtype=jnp.int32))
        return (totals, None)

    totals, _ = lax.scan(conv_one_genome, start_sums, (extended, d_pooled))
    return totals


def query_side(query_rows, grad_rows, key_rows, value_rows):
    heads_q = query_rows.reshape(-1, HEADS, HEAD)
    heads_k = key_rows.reshape(-1, HEADS, HEAD)
    heads_v = value_rows.reshape(-1, HEADS, HEAD)
    heads_g = grad_rows.reshape(-1, HEADS, HEAD)
    scores = jnp.einsum(
        "qhd,khd->hqk", heads_q, heads_k, preferred_element_type=jnp.float32
    ) * HEAD ** (-0.5)
    row_max = jnp.max(scores, axis=-1)
    weights = jnp.exp(scores - row_max[:, :, None])
    row_total = jnp.sum(weights, axis=-1)
    soft_out = weights / row_total[:, :, None]
    soft_half = soft_out.astype(jnp.bfloat16)
    attended = (
        jnp.einsum("hqk,khd->qhd", soft_half, heads_v, preferred_element_type=jnp.float32)
        .reshape(-1, INNER)
        .astype(jnp.bfloat16)
    )
    d_soft = jnp.einsum("qhd,khd->hqk", heads_g, heads_v, preferred_element_type=jnp.float32)
    row_delta = jnp.sum(soft_out * d_soft, axis=-1)
    d_half = (soft_out * (d_soft - row_delta[:, :, None]) * HEAD ** (-0.5)).astype(jnp.bfloat16)
    d_query = (
        jnp.einsum("hqk,khd->qhd", d_half, heads_k, preferred_element_type=jnp.float32)
        .reshape(-1, INNER)
        .astype(jnp.bfloat16)
    )
    return (attended, d_query, soft_half, d_half, row_max, row_total, row_delta)


def attention_side(query_rows, grad_rows, key_rows, value_rows):
    attended, d_query, soft_half, d_half, row_max, row_total, row_delta = query_side(
        query_rows, grad_rows, key_rows, value_rows
    )
    heads_q = query_rows.reshape(-1, HEADS, HEAD)
    heads_g = grad_rows.reshape(-1, HEADS, HEAD)
    d_value = jnp.einsum(
        "hqk,qhd->khd", soft_half, heads_g, preferred_element_type=jnp.float32
    ).reshape(-1, INNER)
    d_key = jnp.einsum("hqk,qhd->khd", d_half, heads_q, preferred_element_type=jnp.float32).reshape(
        -1, INNER
    )
    return (attended, d_query, d_key, d_value)


def per_device(dna_bases, conv_weight, conv_bias, w_query, w_key, w_value, out_grad):
    extended = padded(dna_bases + 1, (("seq", 1),), 2)
    pooled = pooled_rows(extended, conv_weight, conv_bias)
    query_rows = jnp.dot(pooled, w_query, preferred_element_type=jnp.float32).astype(jnp.bfloat16)
    key_rows = jnp.dot(pooled, w_key, preferred_element_type=jnp.float32).astype(jnp.bfloat16)
    value_rows = jnp.dot(pooled, w_value, preferred_element_type=jnp.float32).astype(jnp.bfloat16)
    key_every, value_every = (
        lax.all_gather(key_rows, "seq", axis=1, tiled=True),
        lax.all_gather(value_rows, "seq", axis=1, tiled=True),
    )
    attended, d_query, key_terms, value_terms = jax.vmap(attention_side)(
        query_rows, out_grad, key_every, value_every
    )
    d_key, d_value = (
        lax.psum_scatter(
            key_terms.astype(jnp.bfloat16), "seq", scatter_dimension=1, tiled=True
        ).astype(jnp.float32),
        lax.psum_scatter(
            value_terms.astype(jnp.bfloat16), "seq", scatter_dimension=1, tiled=True
        ).astype(jnp.float32),
    )
    d_key = d_key.astype(jnp.bfloat16)
    d_value = d_value.astype(jnp.bfloat16)
    d_pooled = jnp.einsum("grf,cf->grc", d_query, w_query, preferred_element_type=jnp.float32)
    d_pooled = d_pooled + jnp.einsum(
        "grf,cf->grc", d_key, w_key, preferred_element_type=jnp.float32
    )
    d_pooled = d_pooled + jnp.einsum(
        "grf,cf->grc", d_value, w_value, preferred_element_type=jnp.float32
    )
    conv_part, bias_part = conv_grads(extended, d_pooled, conv_weight, conv_bias)
    conv_grad, bias_grad = lax.psum((conv_part, bias_part), ("dp", "seq"))
    return (attended, pooled, conv_grad.reshape(KERNEL, LETTERS, C), bias_grad)


def solution(mesh):
    in_specs = (P("dp", "seq"), P(), P(), P(), P(), P(), P("dp", "seq", None))
    out_specs = (P("dp", "seq", None), P("dp", "seq", None), P(), P())
    return jax.shard_map(
        per_device, mesh=mesh, in_specs=in_specs, out_specs=out_specs, check_vma=False
    )
```

profile of v0, /device:TPU:1, one launch (start us, length us, event | category | flops | bytes accessed | tf_op | source)
XLA Modules:
  0.0 833.0 jit_solution(14463300207811872843)
XLA Ops:
  7.2 0.8 broadcast_add_fusion
  8.1 1.3 collective-permute-start.1
  9.4 4.6 collective-permute-start
  14.0 0.8 reshape.219
  15.0 7.9 while.41
  16.4 2.5 bitcast_reduce_fusion.2
  20.4 2.5 bitcast_reduce_fusion.2
  22.9 2.2 convolution_convert_fusion.4
  26.1 73.3 %all-gather = bf16[256,768]{1,0:T(8,128)(2,1)S(1)} all-gather(bf16[8,768]{1,0:T(8,128)(2,1)S(1)} %convolution_convert_fusion.6), channel_id=2, replica_groups=mesh['dp'=32,'seq'=32] {'seq'}, dimensions={0}, use_global_device_ids=true | all-gather | bytes 405504 | tf_op jit(solution)/shard_map/all_gather | solution.py:142
  99.6 65.9 %all-gather.1 = bf16[256,768]{1,0:T(8,128)(2,1)} all-gather(bf16[8,768]{1,0:T(8,128)(2,1)S(1)} %convolution_convert_fusion.4), channel_id=3, replica_groups=mesh['dp'=32,'seq'=32] {'seq'}, dimensions={0}, use_global_device_ids=true | all-gather | bytes 405504 | tf_op jit(solution)/shard_map/all_gather | solution.py:141
  165.5 1.2 copy.38
  167.2 1.1 convolution_convert_fusion
  168.2 1.2 convolution_convert_fusion.1
  169.4 3.0 copy.46
  172.4 3.0 copy.44
  175.4 1.3 dynamic-slice
  177.4 0.6 broadcast_in_dim.19
  178.5 0.7 fusion.65
  179.2 325.0 %all-reduce.8.cloned.1.call-done = (bf16[1,256,768]{2,0,1:T(2,128)(2,1)}, bf16[1,256,768]{2,0,1:T(2,128)(2,1)}) async-done(((bf16[1,256,768]{2,0,1:T(2,128)(2,1)}, bf16[1,256,768]{2,0,1:T(2,128)(2,1)}), (bf16[1,256,768]{2,0,1:T(2,128)(2,1)}, bf16[1,256,768]{2,0,1:T(2,128)(2,1)})) %all-reduce.8.cloned.1.call-update) | async-done | bytes 786448
  504.1 0.8 constant_dynamic-slice_fusion
  504.9 2.4 convolution_add_fusion.2
  507.3 2.4 convolution_add_fusion.1
  509.7 12.5 %while.42 = (s32[]{:T(128)}, f32[25,1536]{1,0:T(8,128)S(1)}, f32[1536]{0:T(1024)S(1)}, s32[2]{0:T(128)S(1)}, s32[1028]{0:T(1024)S(1)}, /*index=5*/f32[8,1536]{1,...) while((s32[]{:T(128)}, f32[25,1536]{1,0:T(8,128)S(1)}, ...), condition=%wide.region_10.11_spmd.clone, body=%wide.region_8.10_spmd.clone.sunk | while | flops 291876352 | bytes 7050996 | solution.py:83
  512.0 2.7 fusion.100
  514.7 1.3 convolution_add_fusion.4
  518.2 2.7 fusion.100
  520.9 1.3 convolution_add_fusion.4
  522.3 0.7 reshape.222
  523.3 0.7 convert_element_type.131
  524.0 136.0 %psum.15 = f32[1536]{0:T(1024)} all-reduce(f32[1536]{0:T(1024)S(1)} %get-tuple-element.176), channel_id=1, replica_groups=mesh['dp'=32,'seq'=32] {'dp','seq'}, use_global_device_ids=true, to_apply=%region_12.13 | all-reduce | flops 1536 | bytes 12288 | tf_op jit(solution)/shard_map/psum | solution.py:165
  659.9 164.5 %all-reduce.6.cloned.1.call-done = f32[5,5,1536]{2,1,0:T(8,128)} async-done(((f32[5,5,1536]{2,1,0:T(8,128)}), f32[5,5,1536]{2,1,0:T(8,128)}) %all-reduce.6.cloned.1.call-update) | async-done | bytes 153616 | tf_op jit(solution)/shard_map/psum | solution.py:165
  824.5 1.7 copy.86
  (68 shorter events, 6.1 us)
Async XLA Ops:
  7.2 18.0 %copy-start = (bf16[1536,768]{1,0:T(8,128)(2,1)S(1)}, bf16[1536,768]{1,0:T(8,128)(2,1)}, u32[]{:S(2)}) copy-start(bf16[1536,768]{1,0:T(8,128)(2,1)} %param.14) | copy-start | bytes 7077892
  7.2 496.9 %all-reduce.8.cloned.1.call-start = ((), (), s32[]{:S(2)}) async-start(), calls=%async_computation.1 | async-start | bytes 3145728
  8.1 6.7 collective-permute-start.1
  9.4 5.4 collective-permute-start
  22.9 2.7 copy-start.1
  175.4 649.1 %all-reduce.6.cloned.1.call-start = ((), (), s32[]{:S(2)}) async-start(), calls=%async_computation | async-start | bytes 491520 | tf_op jit(solution)/shard_map/psum | solution.py:165
  178.4 331.2 %copy-start.2 = (bf16[5,5,1536]{2,1,0:T(8,128)(2,1)S(1)}, bf16[5,5,1536]{2,1,0:T(8,128)(2,1)}, u32[]{:S(2)}) copy-start(bf16[5,5,1536]{2,1,0:T(8,128)(2,1)} %get-tuple-element.446) | copy-start | bytes 230404
  178.5 331.3 %copy-start.3 = (f32[1536]{0:T(1024)S(1)}, f32[1536]{0:T(1024)}, u32[]{:S(2)}) copy-start(f32[1536]{0:T(1024)} %get-tuple-element.451) | copy-start | bytes 18436
Sparse Core Ops, SparseCore 0:
  175.5 328.5 all-reduce.7
  523.1 301.3 all-reduce.5
where the time goes:
time: 834 us; the launch traced here: 833 us
  waiting for transfers between devices  490 us (59%)
  blocking collectives  275 us (33%)
  matrix products  24.8 us (3%)
  local copies, waits for them, and re-layouts  17.6 us (2%)
  between operations  14.9 us (2%)
    unnamed x3, waiting for transfers between devices  325 us
    psum x1, waiting for transfers between devices, per_device(): conv_grad, bias_grad = lax.psum((conv_part, bias_part), ('dp', 'seq'))  165 us
    psum x1, blocking collectives, per_device(): conv_grad, bias_grad = lax.psum((conv_part, bias_part), ('dp', 'seq'))  136 us
    all_gather x1, blocking collectives, per_device(): lax.all_gather(value_rows, 'seq', axis=1, tiled=True)  73.3 us
    all_gather x1, blocking collectives, per_device(): lax.all_gather(key_rows, 'seq', axis=1, tiled=True)  65.9 us
  transfers between devices with their start and end apart: 4, of which 2 were waited for; matrix products, arithmetic and copies ran while one was open for 1% of the time, Pallas kernels for 0%

commit v1 on v0

v1 whole, which is shorter than its diff:
```python
import functools

import jax
import jax.numpy as jnp
from jax import lax
from jax.experimental import pallas as pl
from jax.experimental.pallas import tpu as pltpu
from jax.sharding import PartitionSpec as P

C = 1536
HEAD = 192
LETTERS = 5
POOL = 128
INNER = 768
ROWS = 8
SPAN = ROWS * POOL
CODES = 48
WIDE = 256
LANES = 256
DEPTH = 4
RING = 8
SEQ = DEPTH * RING
CHIPS = 16
GELU_A = 0.7978845608028654
GELU_B = 0.044715
NT = (((1,), (1,)), ((), ()))
MESH = pl.DeviceIdType.MESH
F32 = jnp.float32
BF16 = jnp.bfloat16


def window_start(head):
    return 384 * (head // 2) + 128 * (head % 2)


def one_hot_rows(codes):
    width = codes.shape[1]
    wide = jnp.broadcast_to(codes, (8, width))
    letter = lax.broadcasted_iota(jnp.int32, (8, width - 256), 0)
    parts = []
    for tap in range(5):
        moved = wide if tap == 2 else pltpu.roll(wide, (2 - tap) % width, 1)
        hit = moved[:, 128 : width - 128] == letter
        if tap == 0:
            hit = jnp.logical_or(hit, letter >= LETTERS)
        parts.append(jnp.where(hit, 1.0, 0.0).astype(F32))
    parts.append(jnp.zeros_like(parts[0]))
    return jnp.concatenate(parts, axis=0)


def positions_first(rows):
    full = jnp.concatenate([rows, jnp.zeros((128 - CODES, rows.shape[1]), F32)], axis=0)
    blocks = [full[:, at : at + 128].T for at in range(0, rows.shape[1], 128)]
    return jnp.concatenate(blocks, axis=0)


def gelu_twice(x):
    square = x * x
    inner = x * (square * (GELU_A * GELU_B) + GELU_A)
    tanh = jnp.tanh(inner)
    return x + x * tanh, square, tanh


def gelu_slope_twice(x, square, tanh):
    return (1.0 + tanh) + (x - x * (tanh * tanh)) * (square * (3 * GELU_A * GELU_B) + GELU_A)


def stem_kernel(
    dna_hbm, taps_hbm, bias_hbm, wq_hbm, wk_hbm, wv_hbm, grad_hbm,
    attended_ref, pooled_ref, conv_ref, conv_bias_ref,
    dna_ref, taps_ref, bias_ref, grad_ref, weights, table, hot, hot_t, pooled_sum, slopes, halo,
    grad_send, grad_rows, grad_all, pool_rows, qkv_all, back_send, back_rows,
    acc, core_part, tiles, scatter_rows, chip_rows, full,
    load_sem, halo_ss, halo_rs, g1_ss, g1_rs, g2_ss, g2_rs, p_ss, p_rs, q_ss, q_rs, b_ss, b_rs,
    c_ss, c_rs, s_ss, s_rs,
):
    dp = lax.axis_index("dp")
    seq = lax.axis_index("seq")
    head = lax.div(seq, RING)
    col = lax.rem(seq, RING)
    chip = lax.div(dp, 2)
    core = lax.rem(dp, 2)

    def in_seq(index):
        return (dp, index)

    def along_z(step):
        return in_seq(lax.rem(head + (step + DEPTH), DEPTH) * RING + col)

    def along_x(step):
        return in_seq(head * RING + lax.rem(col + step, RING))

    def along_seq(step):
        return in_seq(lax.rem(seq + (step + SEQ), SEQ))

    def along_chips(step):
        return (lax.rem(chip + step, CHIPS) * 2 + core, seq)

    other_core = (chip * 2 + (1 - core), seq)

    def remote(src, dst, ss, rs, device):
        return pltpu.make_async_remote_copy(
            src_ref=src, dst_ref=dst, send_sem=ss, recv_sem=rs, device_id=device, device_id_type=MESH
        )

    small = ((dna_hbm, dna_ref), (taps_hbm, taps_ref), (bias_hbm, bias_ref), (grad_hbm, grad_ref))
    reads = [pltpu.make_async_copy(hbm, ref, load_sem.at[3 + i]) for i, (hbm, ref) in enumerate(small)]
    loads = [
        pltpu.make_async_copy(hbm, weights.at[i], load_sem.at[i])
        for i, hbm in enumerate((wq_hbm, wk_hbm, wv_hbm))
    ]
    for copy in (*reads, *loads):
        copy.start()

    barrier = pltpu.get_barrier_semaphore()

    def greet(device):
        pl.semaphore_signal(barrier, inc=1, device_id=device, device_id_type=MESH)

    def greet_seq(step, _):
        greet(along_seq(step))
        return 0

    def greet_chips(step, _):
        greet(along_chips(step))
        return 0

    lax.fori_loop(1, SEQ, greet_seq, 0)
    lax.fori_loop(1, CHIPS, greet_chips, 0)
    greet(other_core)


    for copy in reads:
        copy.wait()

    bias = bias_ref[...].reshape(1, C)
    bias_high = bias.astype(BF16).astype(F32)
    bias_mid = (bias - bias_high).astype(BF16).astype(F32)
    bias_low = bias - bias_high - bias_mid
    for tap in range(5):
        letters = taps_ref[tap].astype(F32)
        spare = [bias_high, bias_mid, bias_low] if tap == 0 else [jnp.zeros((3, C), F32)]
        pair = jnp.concatenate([letters, *spare], axis=0)
        acc[8 * tap : 8 * tap + 8, :] = pair
    table[0:48, :] = jnp.concatenate([acc[...], jnp.zeros((8, C), F32)], axis=0).astype(BF16)
    table[48:128, :] = jnp.zeros((80, C), BF16)

    codes = dna_ref[...]
    outside = jnp.full((1, 128), -1, jnp.int32)
    rows = one_hot_rows(jnp.concatenate([outside, codes, outside], axis=1))
    hot_t[...] = rows.astype(BF16)
    hot[...] = positions_first(rows).astype(BF16)

    def pre_act(block, lanes):
        return jnp.dot(
            hot[block * POOL : (block + 1) * POOL, :], table[:, lanes], preferred_element_type=F32
        )

    def slope_sums(block, lanes, slope):
        slopes[block, :, lanes] = jnp.dot(
            hot_t[:, block * POOL : (block + 1) * POOL],
            slope.astype(BF16),
            preferred_element_type=F32,
        )

    def lanes_of(part):
        return pl.ds(pl.multiple_of(part * LANES, LANES), LANES)

    def inner_blocks(part, _):
        lanes = lanes_of(part)
        for block in range(1, ROWS - 1):
            x = pre_act(block, lanes)
            twice, square, tanh = gelu_twice(x)
            pooled_sum[block : block + 1, lanes] = jnp.sum(twice, axis=0, keepdims=True)
            slope_sums(block, lanes, gelu_slope_twice(x, square, tanh))
        return 0

    def end_pools(part, _):
        lanes = lanes_of(part)
        for block in (0, ROWS - 1):
            twice, _, _ = gelu_twice(pre_act(block, lanes))
            pooled_sum[block : block + 1, lanes] = jnp.sum(twice, axis=0, keepdims=True)
        return 0

    def end_slopes(part, _):
        lanes = lanes_of(part)
        for block in (0, ROWS - 1):
            x = pre_act(block, lanes)
            _, square, tanh = gelu_twice(x)
            slope_sums(block, lanes, gelu_slope_twice(x, square, tanh))
        return 0

    lane = lax.broadcasted_iota(jnp.int32, (ROWS, WIDE), 1)
    grad = grad_ref[0].astype(F32)
    for h in range(DEPTH):
        low = 64 * (h % 2)
        start = window_start(h)
        keep = jnp.logical_and(lane >= low, lane < low + HEAD)
        window = jnp.where(keep, grad[:, start : start + WIDE], 0.0)
        grad_send[h] = jnp.concatenate([window[:, :128], window[:, 128:]], axis=0).astype(BF16)

    lax.fori_loop(0, C // LANES // 2, inner_blocks, 0)
    pl.semaphore_wait(barrier, SEQ - 1 + CHIPS - 1 + 1)

    halo_sends = [
        remote(dna_ref.at[:, SPAN - 128 : SPAN], halo.at[0], halo_ss.at[0], halo_rs.at[0], along_seq(1)),
        remote(dna_ref.at[:, 0:128], halo.at[1], halo_ss.at[1], halo_rs.at[1], along_seq(-1)),
    ]
    for copy in halo_sends:
        copy.start()
    g1 = [
        remote(
            grad_send.at[lax.rem(head + step, DEPTH)], grad_rows.at[step],
            g1_ss.at[step], g1_rs.at[step], along_z(step),
        )
        for step in range(1, DEPTH)
    ]
    for copy in g1:
        copy.start()
    grad_rows[0] = grad_send[head]

    lax.fori_loop(C // LANES // 2, C // LANES, inner_blocks, 0)

    for copy in halo_sends:
        copy.wait()
    before = jnp.where(seq == 0, -1, halo[0])
    after = jnp.where(seq == SEQ - 1, -1, halo[1])
    first = one_hot_rows(jnp.concatenate([before, codes[:, :256]], axis=1))
    last = one_hot_rows(jnp.concatenate([codes[:, SPAN - 256 :], after], axis=1))
    hot_t[:, :POOL] = first.astype(BF16)
    hot_t[:, SPAN - POOL :] = last.astype(BF16)
    hot[:POOL, :] = positions_first(first).astype(BF16)
    hot[SPAN - POOL :, :] = positions_first(last).astype(BF16)
    lax.fori_loop(0, C // LANES, end_pools, 0)

    pooled = pooled_sum[...] * (0.5 / POOL)
    pooled_ref[0] = pooled.astype(BF16)
    pool_rows[0] = jnp.concatenate([pooled[:, :INNER], pooled[:, INNER:]], axis=0).astype(BF16)
    p1 = [
        remote(pool_rows.at[0], pool_rows.at[step], p_ss.at[step], p_rs.at[step], along_z(step))
        for step in range(1, DEPTH)
    ]
    for copy in p1:
        copy.start()

    for copy in g1:
        copy.wait()
    blocks = grad_rows[...].astype(F32)
    grad_all[0] = jnp.concatenate(
        [jnp.concatenate([blocks[i, :8], blocks[i, 8:]], axis=1) for i in range(DEPTH)], axis=0
    ).astype(BF16)
    g2 = [
        remote(grad_all.at[0], grad_all.at[step], g2_ss.at[step], g2_rs.at[step], along_x(step))
        for step in range(1, RING)
    ]
    for copy in g2:
        copy.start()

    lax.fori_loop(0, C // LANES, end_slopes, 0)

    for load in loads:
        load.wait()
    for copy in p1:
        copy.wait()
    start = pl.multiple_of(384 * lax.div(head, 2) + 128 * lax.rem(head, 2), 128)
    low = 64 * lax.rem(head, 2)
    lane = lax.broadcasted_iota(jnp.int32, (4 * ROWS, WIDE), 1)
    keep = jnp.logical_and(lane >= low, lane < low + HEAD)
    halves = pool_rows[...].reshape(DEPTH * 16, INNER)
    for i in range(3):
        left = jnp.dot(halves, weights[i, :INNER, pl.ds(start, WIDE)], preferred_element_type=F32)
        right = jnp.dot(halves, weights[i, INNER:, pl.ds(start, WIDE)], preferred_element_type=F32)
        rows = jnp.concatenate(
            [left[16 * j : 16 * j + 8] + right[16 * j + 8 : 16 * j + 16] for j in range(DEPTH)], axis=0
        )
        qkv_all[0, 32 * i : 32 * i + 32, :] = jnp.where(keep, rows, 0.0).astype(BF16)
    q1 = [
        remote(qkv_all.at[0], qkv_all.at[step], q_ss.at[step], q_rs.at[step], along_x(step))
        for step in range(1, RING)
    ]
    for copy in q1:
        copy.start()
    for copy in g2:
        copy.wait()
    for copy in q1:
        copy.wait()

    everyone = RING * 32
    q = qkv_all[:, 0:32, :].reshape(everyone, WIDE)
    k = qkv_all[:, 32:64, :].reshape(everyone, WIDE)
    v = qkv_all[:, 64:96, :].reshape(everyone, WIDE)
    g = grad_all[...].reshape(everyone, WIDE)
    scale = HEAD ** (-0.5)

    def soft_parts(scores, d_soft, axis):
        scores = scores * scale
        shifted = jnp.exp(scores - jnp.max(scores, axis=axis, keepdims=True))
        soft = shifted / jnp.sum(shifted, axis=axis, keepdims=True)
        delta = jnp.sum(soft * d_soft, axis=axis, keepdims=True)
        return soft, delta

    def finish(soft, d_soft, delta):
        return soft.astype(BF16), (soft * (d_soft - delta) * scale).astype(BF16)

    scores_t = lax.dot_general(k, q, NT, preferred_element_type=F32)
    d_soft_t = lax.dot_general(v, g, NT, preferred_element_type=F32)
    scores_own = lax.dot_general(q[:32], k, NT, preferred_element_type=F32)
    d_soft_own = lax.dot_general(g[:32], v, NT, preferred_element_type=F32)
    soft_t, delta_t = soft_parts(scores_t, d_soft_t, 0)
    half_t, d_half_t = finish(soft_t[:32], d_soft_t[:32], delta_t)
    soft_own, delta_own = soft_parts(scores_own, d_soft_own, 1)
    half_own, d_half_own = finish(soft_own, d_soft_own, delta_own)
    results = (
        jnp.dot(half_own, v, preferred_element_type=F32),
        jnp.dot(d_half_own, k, preferred_element_type=F32),
        jnp.dot(d_half_t, q, preferred_element_type=F32),
        jnp.dot(half_t, g, preferred_element_type=F32),
    )
    for i in range(DEPTH):
        mine = jnp.concatenate([result[8 * i : 8 * i + 8] for result in results], axis=0).astype(BF16)
        if i == 0:
            back_rows[0] = mine
        else:
            back_send[i] = mine
    b1 = [
        remote(back_send.at[i], back_rows.at[i], b_ss.at[i], b_rs.at[i], along_z(-i))
        for i in range(1, DEPTH)
    ]
    for copy in b1:
        copy.start()
    for copy in b1:
        copy.wait()

    by_head = [back_rows[lax.rem(h - head + DEPTH, DEPTH)].astype(F32) for h in range(DEPTH)]

    def joined(i):
        a, b, c, d = (rows[8 * i : 8 * i + 8] for rows in by_head)
        return jnp.concatenate(
            [a[:, :128], a[:, 128:] + b[:, :128], b[:, 128:], c[:, :128], c[:, 128:] + d[:, :128], d[:, 128:]],
            axis=1,
        ).astype(BF16)

    attended_ref[0] = joined(0)
    d_pooled = lax.dot_general(joined(1), weights[0], NT, preferred_element_type=F32)
    d_pooled += lax.dot_general(joined(2), weights[1], NT, preferred_element_type=F32)
    d_pooled += lax.dot_general(joined(3), weights[2], NT, preferred_element_type=F32)
    d_pooled *= 0.5 / POOL
    total = slopes[0, 0:40, :] * d_pooled[0:1]
    for block in range(1, ROWS):
        total += slopes[block, 0:40, :] * d_pooled[block : block + 1]
    acc[...] = total

    half = C // 2
    theirs = pl.ds(pl.multiple_of((1 - core) * half, 128), half)
    ours = pl.ds(pl.multiple_of(core * half, 128), half)
    swap = remote(acc.at[:, theirs], core_part, c_ss.at[0], c_rs.at[0], other_core)
    swap.start()
    swap.wait()
    both = acc[:, ours] + core_part[...]
    for tap in range(5):
        for part in range(6):
            tiles[6 * tap + part] = both[8 * tap : 8 * tap + 8, 128 * part : 128 * part + 128]
    tiles[30:32] = jnp.zeros((2, 8, 128), F32)

    def scatter(step, _):
        to = lax.rem(seq + step, SEQ)
        remote(tiles.at[to], scatter_rows.at[step], s_ss.at[0], s_rs.at[0], in_seq(to)).start()
        return 0

    def spread(step, _):
        remote(chip_rows.at[0], chip_rows.at[step], s_ss.at[1], s_rs.at[1], along_chips(step)).start()
        return 0

    def gather(step, _):
        mine = full.at[core, seq]
        remote(mine, mine, s_ss.at[2], s_rs.at[2], along_seq(step)).start()
        return 0

    lax.fori_loop(1, SEQ, scatter, 0)
    arrived = scatter_rows.at[1:SEQ]
    remote(arrived, arrived, s_ss.at[0], s_rs.at[0], other_core).wait()
    chip_rows[0] = tiles[seq] + jnp.sum(scatter_rows[1:SEQ], axis=0)
    lax.fori_loop(1, CHIPS, spread, 0)
    arrived = chip_rows.at[1:CHIPS]
    remote(arrived, arrived, s_ss.at[1], s_rs.at[1], other_core).wait()
    tile = chip_rows[chip]
    for i in range(1, CHIPS):
        tile += chip_rows[lax.rem(chip + (CHIPS - i), CHIPS)]
    full[core, seq] = tile
    lax.fori_loop(1, SEQ, gather, 0)
    arrived = full.at[core, 0 : SEQ - 1]
    remote(arrived, arrived, s_ss.at[2], s_rs.at[2], other_core).wait()
    swap = remote(full.at[core], full.at[core], c_ss.at[1], c_rs.at[1], other_core)
    swap.start()
    swap.wait()
    for side in range(2):
        for tap in range(5):
            for part in range(6):
                lanes = slice(half * side + 128 * part, half * side + 128 * part + 128)
                conv_ref[tap, :, lanes] = full[side, 6 * tap + part, 0:LETTERS, :]
                if tap == 0:
                    conv_bias_ref[lanes] = full[side, part, LETTERS, :]


def per_device(dna_bases, conv_weight, conv_bias, w_query, w_key, w_value, out_grad):
    vmem = pl.BlockSpec(memory_space=pltpu.VMEM)
    hbm = pl.BlockSpec(memory_space=pl.ANY)
    dma = pltpu.SemaphoreType.DMA
    return pl.pallas_call(
        stem_kernel,
        name="genomic_stem",
        out_shape=(
            jax.ShapeDtypeStruct((1, ROWS, INNER), BF16),
            jax.ShapeDtypeStruct((1, ROWS, C), BF16),
            jax.ShapeDtypeStruct((5, LETTERS, C), F32),
            jax.ShapeDtypeStruct((C,), F32),
        ),
        in_specs=[hbm] * 7,
        out_specs=(vmem, vmem, vmem, vmem),
        scratch_shapes=[
            pltpu.VMEM((1, SPAN), jnp.int32),
            pltpu.VMEM((5, LETTERS, C), BF16),
            pltpu.VMEM((C,), F32),
            pltpu.VMEM((1, ROWS, INNER), BF16),
            pltpu.VMEM((3, C, INNER), BF16),
            pltpu.VMEM((128, C), BF16),
            pltpu.VMEM((SPAN, 128), BF16),
            pltpu.VMEM((CODES, SPAN), BF16),
            pltpu.VMEM((ROWS, C), F32),
            pltpu.VMEM((ROWS, CODES, C), F32),
            pltpu.VMEM((2, 1, 128), jnp.int32),
            pltpu.VMEM((DEPTH, 16, 128), BF16),
            pltpu.VMEM((DEPTH, 16, 128), BF16),
            pltpu.VMEM((RING, 32, WIDE), BF16),
            pltpu.VMEM((DEPTH, 16, INNER), BF16),
            pltpu.VMEM((RING, 96, WIDE), BF16),
            pltpu.VMEM((DEPTH, 32, WIDE), BF16),
            pltpu.VMEM((DEPTH, 32, WIDE), BF16),
            pltpu.VMEM((40, C), F32),
            pltpu.VMEM((40, C // 2), F32),
            pltpu.VMEM((SEQ, 8, 128), F32),
            pltpu.VMEM((SEQ, 8, 128), F32),
            pltpu.VMEM((CHIPS, 8, 128), F32),
            pltpu.VMEM((2, SEQ, 8, 128), F32),
            dma((7,)), dma((2,)), dma((2,)),
            dma((DEPTH,)), dma((DEPTH,)), dma((RING,)), dma((RING,)), dma((DEPTH,)), dma((DEPTH,)),
            dma((RING,)), dma((RING,)), dma((DEPTH,)), dma((DEPTH,)),
            dma((2,)), dma((2,)), dma((3,)), dma((3,)),
        ],
        compiler_params=pltpu.CompilerParams(
            collective_id=0, has_side_effects=True, vmem_limit_bytes=60 * 2**20
        ),
        cost_estimate=pl.CostEstimate(
            flops=2_000_000_000, bytes_accessed=8_000_000, transcendentals=4_000_000
        ),
    )(
        dna_bases, conv_weight, conv_bias, w_query, w_key, w_value, out_grad,
    )


def solution(mesh):
    in_specs = (P("dp", "seq"), P(), P(), P(), P(), P(), P("dp", "seq", None))
    out_specs = (P("dp", "seq", None), P("dp", "seq", None), P(), P())
    return jax.shard_map(
        per_device, mesh=mesh, in_specs=in_specs, out_specs=out_specs, check_vma=False
    )
```

time: 834 us -> 86.8 us (0.10)
  waiting for transfers between devices: 490 us -> 0 us
  blocking collectives: 275 us -> 0 us
  Pallas kernels: 0 us -> 80.2 us
  matrix products: 24.8 us -> 0 us
  between operations: 14.9 us -> 0.64 us
  local copies, waits for them, and re-layouts: 17.6 us -> 5.6 us
    unnamed x3 -> x0, waiting for transfers between devices: 325 us -> none
    psum x1 -> x0, waiting for transfers between devices: 165 us -> none  [per_device(): conv_grad, bias_grad = lax.psum((conv_part, bias_part), ('dp', 'seq'))]
    all_gather x2 -> x0, blocking collectives: 139 us -> none  [the longest x1 73.3 us: per_device(): lax.all_gather(value_rows, 'seq', axis=1, tiled=True)]
    psum x1 -> x0, blocking collectives: 136 us -> none  [per_device(): conv_grad, bias_grad = lax.psum((conv_part, bias_part), ('dp', 'seq'))]
    pallas_call x0 -> x1, Pallas kernels: none -> 80.2 us  [per_device(): pl.pallas_call(stem_kernel, name='genomic_stem', out_shape=(jax.ShapeDtyp...]
    dot_general x17 -> x0, matrix products: 24.4 us -> none  [the longest x4 10.3 us: conv_pre(): jnp.dot(one_hot.astype(jnp.bfloat16), tap_table, preferred_element_type=j...]
  transfers between devices with their start and end apart: 4 -> 0, of which waited for: 2 -> 0; matrix products, arithmetic and copies ran while one was open for 1% -> 0% of each run, Pallas kernels for 0% -> 0%
where the time goes in v1:
time: 86.8 us; the launch traced here: 86.5 us
  Pallas kernels  80.2 us (92%)
  local copies, waits for them, and re-layouts  5.6 us (6%)
    pallas_call x1, Pallas kernels, per_device(): pl.pallas_call(stem_kernel, name='genomic_stem', out_shape=(jax.ShapeDtyp...  80.2 us
    unnamed x4, local copies, waits for them, and re-layouts  5.6 us

profile of v1, /device:TPU:1, one launch (start us, length us, event | category | flops | bytes accessed | tf_op | source)
XLA Modules:
  0.0 86.5 jit_solution(8708362058561988869)
XLA Ops:
  0.6 80.2 %genomic_stem.1 = (bf16[1,8,768]{2,1,0:T(8,128)(2,1)}, bf16[1,8,1536]{2,1,0:T(8,128)(2,1)}, f32[5,5,1536]{2,1,0:T(8,128)}, f32[1536]{0:T(1024)}) custom-call(s32[1,1024]{1,0:T(1,128)} %dna_hbm.1, bf16[5,5,1536]{2,1,0:T(8,128)(2,1)} %taps_hbm.1, f32[1536]{0:T(1024)} %bias_hbm.1, bf16[1536,768]{1,0:T(8,128)(2,1)} %wq_hbm.1, bf16[1536,768]{1,0:T(8,128)(2,1)} %wk_hbm.1, ...), custom_call_target="tpu_custom_call" | custom-call | flops 2000000000 | bytes 8000000 | tf_op jit(solution)/shard_map/genomic_stem/pallas_call | solution.py:409
  80.9 1.3 %copy.15 = bf16[1,8,768]{2,1,0:T(8,128)(2,1)} copy(bf16[1,8,768]{2,1,0:T(8,128)(2,1)} %get-tuple-element.8) | data formatting | bytes 24576
  82.2 1.3 %copy.16 = bf16[1,8,1536]{2,1,0:T(8,128)(2,1)} copy(bf16[1,8,1536]{2,1,0:T(8,128)(2,1)} %get-tuple-element.9) | data formatting | bytes 49152
  83.5 1.7 %copy.17 = f32[5,5,1536]{2,1,0:T(8,128)} copy(f32[5,5,1536]{2,1,0:T(8,128)} %get-tuple-element.10) | data formatting | bytes 307200
  85.2 1.3 %copy.18 = f32[1536]{0:T(1024)} copy(f32[1536]{0:T(1024)} %get-tuple-element.11) | data formatting | bytes 12288

commit v2 on v1

v2 whole, which is shorter than its diff:
```python
import functools

import jax
import jax.numpy as jnp
from jax import lax
from jax.experimental import pallas as pl
from jax.experimental.pallas import tpu as pltpu
from jax.sharding import PartitionSpec as P

C = 1536
HEAD = 192
LETTERS = 5
POOL = 128
INNER = 768
ROWS = 8
SPAN = ROWS * POOL
CODES = 48
WIDE = 256
LANES = 512
DEPTH = 4
RING = 8
SEQ = DEPTH * RING
NEAR = 32
FAR = 32
GELU_A = 0.7978845608028654
GELU_B = 0.044715
NT = (((1,), (1,)), ((), ()))
MESH = pl.DeviceIdType.MESH
F32 = jnp.float32
BF16 = jnp.bfloat16


def bits(value, low, count):
    return lax.bitwise_and(lax.shift_right_logical(value, low), (1 << count) - 1)


def window_start(head):
    return 384 * (head // 2) + 128 * (head % 2)


def one_hot_rows(codes):
    width = codes.shape[1]
    wide = jnp.broadcast_to(codes, (8, width))
    letter = lax.broadcasted_iota(jnp.int32, (8, width - 256), 0)
    parts = []
    for tap in range(5):
        moved = wide if tap == 2 else pltpu.roll(wide, (2 - tap) % width, 1)
        hit = moved[:, 128 : width - 128] == letter
        if tap == 0:
            hit = jnp.logical_or(hit, letter >= LETTERS)
        parts.append(jnp.where(hit, 1.0, 0.0).astype(F32))
    parts.append(jnp.zeros_like(parts[0]))
    return jnp.concatenate(parts, axis=0)


def positions_first(rows):
    full = jnp.concatenate([rows, jnp.zeros((128 - CODES, rows.shape[1]), F32)], axis=0)
    blocks = [full[:, at : at + 128].T for at in range(0, rows.shape[1], 128)]
    return jnp.concatenate(blocks, axis=0)


def gelu_twice(x):
    square = x * x
    inner = x * (square * (GELU_A * GELU_B) + GELU_A)
    tanh = jnp.tanh(inner)
    return x + x * tanh, square, tanh


def gelu_slope_twice(x, square, tanh):
    return (1.0 + tanh) + (x - x * (tanh * tanh)) * (square * (3 * GELU_A * GELU_B) + GELU_A)


def stem_kernel(
    dna_hbm, taps_hbm, bias_hbm, wq_hbm, wk_hbm, wv_hbm, grad_hbm,
    attended_ref, pooled_ref, conv_ref, conv_bias_ref,
    dna_ref, taps_ref, bias_ref, grad_ref, weights, table, hot, hot_t, pooled_sum, slope_rows, slopes, halo,
    grad_send, grad_rows, grad_all, pool_rows, k_all, qv_all, back_send, back_rows,
    acc, chunks, near_rows, far_rows, full,
    load_sem, halo_ss, halo_rs, g1_ss, g1_rs, g2_ss, g2_rs, p_ss, p_rs, k_ss, k_rs, q_ss, q_rs, b_ss, b_rs,
    s_ss, s_rs,
):
    dp = lax.axis_index("dp")
    seq = lax.axis_index("seq")
    head, col = bits(seq, 3, 2), bits(seq, 0, 3)
    near = col * 4 + bits(dp, 0, 2)
    far = bits(dp, 2, 2) * 8 + bits(dp, 4, 1) * 4 + head

    def along_z(step):
        return (dp, lax.bitwise_and(seq + (step * RING + SEQ), SEQ - 1))

    def along_x(step):
        return (dp, head * RING + lax.bitwise_and(col + step, RING - 1))

    def along_seq(step):
        return (dp, lax.bitwise_and(seq + (step + SEQ), SEQ - 1))

    def device_at(near, far):
        return (
            bits(far, 2, 1) * 16 + bits(far, 3, 2) * 4 + bits(near, 0, 2),
            bits(far, 0, 2) * RING + bits(near, 2, 3),
        )

    def along_near(step):
        to = lax.bitwise_and(near + step, NEAR - 1)
        return to, device_at(to, far)

    def along_far(step):
        return device_at(near, lax.bitwise_and(far + step, FAR - 1))

    def remote(src, dst, ss, rs, device):
        return pltpu.make_async_remote_copy(
            src_ref=src, dst_ref=dst, send_sem=ss, recv_sem=rs, device_id=device, device_id_type=MESH
        )

    barrier = pltpu.get_barrier_semaphore()

    def greet(device):
        pl.semaphore_signal(barrier, inc=1, device_id=device, device_id_type=MESH)

    def greet_near(step, _):
        greet(along_near(step)[1])
        return 0

    def greet_far(step, _):
        greet(along_far(step))
        return 0

    greet(along_seq(1))
    greet(along_seq(-1))
    for step in (2, 1, 3):
        greet(along_z(step))
    for step in range(1, RING):
        greet(along_x(step))
    lax.fori_loop(1, NEAR, greet_near, 0)
    lax.fori_loop(1, FAR, greet_far, 0)


    small = ((dna_hbm, dna_ref), (taps_hbm, taps_ref), (bias_hbm, bias_ref), (grad_hbm, grad_ref))
    reads = [pltpu.make_async_copy(hbm, ref, load_sem.at[3 + i]) for i, (hbm, ref) in enumerate(small)]
    loads = [
        pltpu.make_async_copy(hbm, weights.at[i], load_sem.at[i])
        for i, hbm in enumerate((wq_hbm, wk_hbm, wv_hbm))
    ]
    for copy in (*reads, *loads):
        copy.start()

    for copy in reads:
        copy.wait()

    bias = bias_ref[...].reshape(1, C)
    bias_high = bias.astype(BF16).astype(F32)
    bias_mid = (bias - bias_high).astype(BF16).astype(F32)
    bias_low = bias - bias_high - bias_mid
    for tap in range(5):
        letters = taps_ref[tap].astype(F32)
        spare = [bias_high, bias_mid, bias_low] if tap == 0 else [jnp.zeros((3, C), F32)]
        pair = jnp.concatenate([letters, *spare], axis=0)
        acc[8 * tap : 8 * tap + 8, :] = pair
    table[0:48, :] = jnp.concatenate([acc[...], jnp.zeros((8, C), F32)], axis=0).astype(BF16)
    table[48:128, :] = jnp.zeros((80, C), BF16)

    codes = dna_ref[...]
    outside = jnp.full((1, 128), -1, jnp.int32)
    rows = one_hot_rows(jnp.concatenate([outside, codes, outside], axis=1))
    hot_t[...] = rows.astype(BF16)
    hot[...] = positions_first(rows).astype(BF16)

    def pre_act(block, lanes):
        return jnp.dot(
            hot[block * POOL : (block + 1) * POOL, :], table[:, lanes], preferred_element_type=F32
        )

    def lanes_of(part):
        return pl.ds(pl.multiple_of(part * LANES, LANES), LANES)

    def pools(blocks):
        def body(part, _):
            lanes = lanes_of(part)
            for block in blocks:
                twice, _, _ = gelu_twice(pre_act(block, lanes))
                pooled_sum[block : block + 1, lanes] = jnp.sum(twice, axis=0, keepdims=True)
            return 0

        return body

    inner, ends = pools(range(1, ROWS - 1)), pools((0, ROWS - 1))

    def slope_part(part, _):
        lanes = lanes_of(part)
        for block in range(ROWS):
            x = pre_act(block, lanes)
            _, square, tanh = gelu_twice(x)
            slope = gelu_slope_twice(x, square, tanh)
            slope_rows[block * POOL : (block + 1) * POOL, lanes] = slope.astype(BF16)
        return 0

    lane = lax.broadcasted_iota(jnp.int32, (ROWS, WIDE), 1)
    grad = grad_ref[0].astype(F32)
    for h in range(DEPTH):
        low = 64 * (h % 2)
        start = window_start(h)
        keep = jnp.logical_and(lane >= low, lane < low + HEAD)
        window = jnp.where(keep, grad[:, start : start + WIDE], 0.0)
        if h % 2 == 0:
            window = pltpu.roll(window, 64, 1)
        grad_send[h] = jnp.concatenate([window[:, :128], window[:, 128:]], axis=0).astype(BF16)

    lax.fori_loop(0, 1, inner, 0)
    pl.semaphore_wait(barrier, 2 + (DEPTH - 1) + (RING - 1) + (NEAR - 1) + (FAR - 1))

    halo_sends = [
        remote(dna_ref.at[:, SPAN - 128 : SPAN], halo.at[0], halo_ss.at[0], halo_rs.at[0], along_seq(1)),
        remote(dna_ref.at[:, 0:128], halo.at[1], halo_ss.at[1], halo_rs.at[1], along_seq(-1)),
    ]
    for copy in halo_sends:
        copy.start()
    g1 = [
        remote(
            grad_send.at[lax.bitwise_and(head + step, DEPTH - 1)], grad_rows.at[step],
            g1_ss.at[step], g1_rs.at[step], along_z(step),
        )
        for step in range(1, DEPTH)
    ]
    for copy in g1:
        copy.start()
    grad_rows[0] = grad_send[head]

    lax.fori_loop(1, C // LANES, inner, 0)

    for copy in halo_sends:
        copy.wait()
    before = jnp.where(seq == 0, -1, halo[0])
    after = jnp.where(seq == SEQ - 1, -1, halo[1])
    first = one_hot_rows(jnp.concatenate([before, codes[:, :256]], axis=1))
    last = one_hot_rows(jnp.concatenate([codes[:, SPAN - 256 :], after], axis=1))
    hot_t[:, :POOL] = first.astype(BF16)
    hot_t[:, SPAN - POOL :] = last.astype(BF16)
    hot[:POOL, :] = positions_first(first).astype(BF16)
    hot[SPAN - POOL :, :] = positions_first(last).astype(BF16)
    lax.fori_loop(0, C // LANES, ends, 0)

    pooled = pooled_sum[...] * (0.5 / POOL)
    pooled_ref[0] = pooled.astype(BF16)
    pool_rows[0] = jnp.concatenate([pooled[:, :INNER], pooled[:, INNER:]], axis=0).astype(BF16)
    p1 = [
        remote(pool_rows.at[0], pool_rows.at[step], p_ss.at[step], p_rs.at[step], along_z(step))
        for step in range(1, DEPTH)
    ]
    for copy in p1:
        copy.start()

    for copy in g1:
        copy.wait()
    blocks = grad_rows[...].astype(F32)
    grad_all[0] = jnp.concatenate(
        [jnp.concatenate([blocks[i, :8], blocks[i, 8:]], axis=1) for i in range(DEPTH)], axis=0
    ).astype(BF16)
    g2 = [
        remote(grad_all.at[0], grad_all.at[step], g2_ss.at[step], g2_rs.at[step], along_x(step))
        for step in range(1, RING)
    ]
    for copy in g2:
        copy.start()

    lax.fori_loop(0, C // LANES - 1, slope_part, 0)

    for load in loads:
        load.wait()
    for copy in p1:
        copy.wait()
    odd = bits(head, 0, 1)
    start = pl.multiple_of(384 * bits(head, 1, 1) + 128 * odd, 128)
    low = 64 * odd
    lane = lax.broadcasted_iota(jnp.int32, (4 * ROWS, WIDE), 1)
    keep = jnp.logical_and(lane >= low, lane < low + HEAD)
    halves = pool_rows[...].reshape(DEPTH * 16, INNER)

    def projected(i):
        left = jnp.dot(halves, weights[i, :INNER, pl.ds(start, WIDE)], preferred_element_type=F32)
        right = jnp.dot(halves, weights[i, INNER:, pl.ds(start, WIDE)], preferred_element_type=F32)
        rows = jnp.concatenate(
            [left[16 * j : 16 * j + 8] + right[16 * j + 8 : 16 * j + 16] for j in range(DEPTH)], axis=0
        )
        return pltpu.roll(jnp.where(keep, rows, 0.0), 192 * odd, 1)

    def round_x(ref, ss, rs):
        copies = [
            remote(ref.at[0], ref.at[step], ss.at[step], rs.at[step], along_x(step))
            for step in (4, 3, 5, 2, 6, 1, 7)
        ]
        for copy in copies:
            copy.start()
        return copies

    k_all[0] = projected(1).astype(BF16)
    k1 = round_x(k_all, k_ss, k_rs)
    query, value = projected(0), pltpu.roll(projected(2), 64, 1)
    qv_all[0] = jnp.concatenate(
        [query[:, :128], query[:, 128:] + value[:, :128], value[:, 128:]], axis=1
    ).astype(BF16)
    q1 = round_x(qv_all, q_ss, q_rs) + k1
    lax.fori_loop(C // LANES - 1, C // LANES, slope_part, 0)
    for block in range(ROWS):
        rows = slice(block * POOL, (block + 1) * POOL)
        slopes[block] = jnp.dot(hot_t[:, rows], slope_rows[rows, :], preferred_element_type=F32)
    for copy in g2:
        copy.wait()
    for copy in q1:
        copy.wait()

    everyone = RING * 32
    q = qv_all[:, :, :WIDE].reshape(everyone, WIDE)
    v = qv_all[:, :, 128:].reshape(everyone, WIDE)
    k = k_all[...].reshape(everyone, WIDE)
    g = grad_all[...].reshape(everyone, WIDE)
    scale = HEAD ** (-0.5)

    def soft_parts(scores, d_soft, axis):
        scores = scores * scale
        shifted = jnp.exp(scores - jnp.max(scores, axis=axis, keepdims=True))
        soft = shifted / jnp.sum(shifted, axis=axis, keepdims=True)
        delta = jnp.sum(soft * d_soft, axis=axis, keepdims=True)
        return soft, delta

    def finish(soft, d_soft, delta):
        return soft.astype(BF16), (soft * (d_soft - delta) * scale).astype(BF16)

    scores_t = lax.dot_general(k, q, NT, preferred_element_type=F32)
    d_soft_t = lax.dot_general(v, g, NT, preferred_element_type=F32)
    scores_own = lax.dot_general(q[:32], k, NT, preferred_element_type=F32)
    d_soft_own = lax.dot_general(g[:32], v, NT, preferred_element_type=F32)
    soft_t, delta_t = soft_parts(scores_t, d_soft_t, 0)
    half_t, d_half_t = finish(soft_t[:32], d_soft_t[:32], delta_t)
    soft_own, delta_own = soft_parts(scores_own, d_soft_own, 1)
    half_own, d_half_own = finish(soft_own, d_soft_own, delta_own)
    results = (
        jnp.dot(half_own, v, preferred_element_type=F32),
        jnp.dot(d_half_own, k, preferred_element_type=F32),
        jnp.dot(d_half_t, q, preferred_element_type=F32),
        jnp.dot(half_t, g, preferred_element_type=F32),
    )
    low_side, high_side = 64 * odd, 192 * (1 - odd)
    results = (
        pltpu.roll(jnp.where(lane >= 64, results[0], 0.0), high_side, 1),
        pltpu.roll(results[1], low_side, 1),
        pltpu.roll(jnp.where(lane < HEAD, results[2], 0.0), low_side, 1),
        pltpu.roll(results[3], high_side, 1),
    )
    for i in range(DEPTH):
        mine = jnp.concatenate([result[8 * i : 8 * i + 8] for result in results], axis=0).astype(BF16)
        if i == 0:
            back_rows[0] = mine
        else:
            back_send[i] = mine
    b1 = [
        remote(back_send.at[i], back_rows.at[i], b_ss.at[i], b_rs.at[i], along_z(-i))
        for i in range(1, DEPTH)
    ]
    for copy in b1:
        copy.start()
    for copy in b1:
        copy.wait()

    by_head = [back_rows[lax.bitwise_and(h - head + DEPTH, DEPTH - 1)].astype(F32) for h in range(DEPTH)]

    def joined(i):
        a, b, c, d = (rows[8 * i : 8 * i + 8] for rows in by_head)
        return jnp.concatenate(
            [a[:, :128], a[:, 128:] + b[:, :128], b[:, 128:], c[:, :128], c[:, 128:] + d[:, :128], d[:, 128:]],
            axis=1,
        ).astype(BF16)

    attended_ref[0] = joined(0)
    d_pooled = lax.dot_general(joined(1), weights[0], NT, preferred_element_type=F32)
    d_pooled += lax.dot_general(joined(2), weights[1], NT, preferred_element_type=F32)
    d_pooled += lax.dot_general(joined(3), weights[2], NT, preferred_element_type=F32)
    d_pooled *= 0.5 / POOL
    total = slopes[0, 0:40, :] * d_pooled[0:1]
    for block in range(1, ROWS):
        total += slopes[block, 0:40, :] * d_pooled[block : block + 1]
    for tap in range(5):
        for part in range(6):
            rows, at = slice(8 * tap, 8 * tap + 8), 256 * part
            chunk = [total[rows, at : at + 128], total[rows, at + 128 : at + 256]]
            chunks[6 * tap + part] = jnp.concatenate(chunk, axis=0).astype(BF16)
    chunks[30:32] = jnp.zeros((2, 16, 128), BF16)

    def scatter(step, _):
        to, device = along_near(step)
        remote(chunks.at[to], near_rows.at[step], s_ss.at[0], s_rs.at[0], device).start()
        return 0

    def spread(step, _):
        remote(far_rows.at[0], far_rows.at[step], s_ss.at[1], s_rs.at[1], along_far(step)).start()
        return 0

    def gather(step, _):
        mine = full.at[near]
        remote(mine, mine, s_ss.at[2], s_rs.at[2], along_near(step)[1]).start()
        return 0

    def wait_all(ref, at):
        remote(ref, ref, s_ss.at[at], s_rs.at[at], along_z(1)).wait()

    lax.fori_loop(1, NEAR, scatter, 0)
    wait_all(near_rows.at[1:NEAR], 0)
    near_sum = chunks[near].astype(F32) + jnp.sum(near_rows[1:NEAR].astype(F32), axis=0)
    far_rows[0] = near_sum.astype(BF16)
    lax.fori_loop(1, FAR, spread, 0)
    wait_all(far_rows.at[1:FAR], 1)
    far_sum = far_rows[far].astype(F32)
    for i in range(1, FAR):
        far_sum += far_rows[lax.bitwise_and(far + (FAR - i), FAR - 1)].astype(F32)
    full[near] = far_sum.astype(BF16)
    lax.fori_loop(1, NEAR, gather, 0)
    wait_all(full.at[0 : NEAR - 1], 2)
    for tap in range(5):
        for part in range(6):
            chunk = full[6 * tap + part].astype(F32)
            for side in range(2):
                lanes = slice(256 * part + 128 * side, 256 * part + 128 * side + 128)
                conv_ref[tap, :, lanes] = chunk[8 * side : 8 * side + LETTERS]
                if tap == 0:
                    conv_bias_ref[lanes] = chunk[8 * side + LETTERS]


def write_kernel(*refs):
    count = len(refs) // 2
    sems = refs[-1]
    copies = [pltpu.make_async_copy(refs[i], refs[count + i], sems.at[i]) for i in range(count)]
    for copy in copies:
        copy.start()
    for copy in copies:
        copy.wait()


def per_device(dna_bases, conv_weight, conv_bias, w_query, w_key, w_value, out_grad):
    vmem = pl.BlockSpec(memory_space=pltpu.VMEM)
    hbm = pl.BlockSpec(memory_space=pltpu.HBM)
    dma = pltpu.SemaphoreType.DMA
    results = pl.pallas_call(
        stem_kernel,
        name="genomic_stem",
        out_shape=(
            jax.ShapeDtypeStruct((1, ROWS, INNER), BF16),
            jax.ShapeDtypeStruct((1, ROWS, C), BF16),
            jax.ShapeDtypeStruct((5, LETTERS, C), F32),
            jax.ShapeDtypeStruct((C,), F32),
        ),
        in_specs=[hbm] * 7,
        out_specs=(vmem, vmem, vmem, vmem),
        scratch_shapes=[
            pltpu.VMEM((1, SPAN), jnp.int32),
            pltpu.VMEM((5, LETTERS, C), BF16),
            pltpu.VMEM((C,), F32),
            pltpu.VMEM((1, ROWS, INNER), BF16),
            pltpu.VMEM((3, C, INNER), BF16),
            pltpu.VMEM((128, C), BF16),
            pltpu.VMEM((SPAN, 128), BF16),
            pltpu.VMEM((CODES, SPAN), BF16),
            pltpu.VMEM((ROWS, C), F32),
            pltpu.VMEM((SPAN, C), BF16),
            pltpu.VMEM((ROWS, CODES, C), F32),
            pltpu.VMEM((2, 1, 128), jnp.int32),
            pltpu.VMEM((DEPTH, 16, 128), BF16),
            pltpu.VMEM((DEPTH, 16, 128), BF16),
            pltpu.VMEM((RING, 32, WIDE), BF16),
            pltpu.VMEM((DEPTH, 16, INNER), BF16),
            pltpu.VMEM((RING, 32, WIDE), BF16),
            pltpu.VMEM((RING, 32, 384), BF16),
            pltpu.VMEM((DEPTH, 32, WIDE), BF16),
            pltpu.VMEM((DEPTH, 32, WIDE), BF16),
            pltpu.VMEM((40, C), F32),
            pltpu.VMEM((NEAR, 16, 128), BF16),
            pltpu.VMEM((NEAR, 16, 128), BF16),
            pltpu.VMEM((FAR, 16, 128), BF16),
            pltpu.VMEM((NEAR, 16, 128), BF16),
            dma((7,)), dma((2,)), dma((2,)),
            dma((DEPTH,)), dma((DEPTH,)), dma((RING,)), dma((RING,)), dma((DEPTH,)), dma((DEPTH,)),
            dma((RING,)), dma((RING,)), dma((RING,)), dma((RING,)), dma((DEPTH,)), dma((DEPTH,)),
            dma((3,)), dma((3,)),
        ],
        compiler_params=pltpu.CompilerParams(
            collective_id=0, has_side_effects=True, vmem_limit_bytes=48 * 2**20
        ),
        cost_estimate=pl.CostEstimate(
            flops=2_000_000_000, bytes_accessed=8_000_000, transcendentals=4_000_000
        ),
    )(
        *(pltpu.with_memory_space_constraint(a, pltpu.HBM) for a in (
        dna_bases, conv_weight, conv_bias, w_query, w_key, w_value, out_grad))
    )
    return pl.pallas_call(
        write_kernel,
        name="write_results",
        out_shape=tuple(jax.ShapeDtypeStruct(a.shape, a.dtype) for a in results),
        in_specs=[vmem] * 4,
        out_specs=(hbm,) * 4,
        scratch_shapes=[dma((4,))],
        compiler_params=pltpu.CompilerParams(vmem_limit_bytes=2**20),
    )(*results)


def solution(mesh):
    in_specs = (P("dp", "seq"), P(), P(), P(), P(), P(), P("dp", "seq", None))
    out_specs = (P("dp", "seq", None), P("dp", "seq", None), P(), P())
    return jax.shard_map(
        per_device, mesh=mesh, in_specs=in_specs, out_specs=out_specs, check_vma=False
    )
```

time: 86.8 us -> 69.7 us (0.80)
  Pallas kernels: 80.2 us -> 68.9 us
  local copies, waits for them, and re-layouts: 5.6 us -> 0 us
    pallas_call x1, Pallas kernels: 80.2 us -> 68.2 us  [per_device(): pl.pallas_call(stem_kernel, name='genomic_stem', out_shape=(jax.ShapeDtyp...]
    unnamed x4 -> x0, local copies, waits for them, and re-layouts: 5.6 us -> none
where the time goes in v2:
time: 69.7 us; the launch traced here: 69.6 us
  Pallas kernels  68.9 us (99%)
    pallas_call x1, Pallas kernels, per_device(): pl.pallas_call(stem_kernel, name='genomic_stem', out_shape=(jax.ShapeDtyp...  68.2 us

profile of v2, /device:TPU:1, one launch (start us, length us, event | category | flops | bytes accessed | tf_op | source)
XLA Modules:
  0.0 69.6 jit_solution(507279224732022507)
XLA Ops:
  0.6 68.2 %genomic_stem.1 = (bf16[1,8,768]{2,1,0:T(8,128)(2,1)S(1)}, bf16[1,8,1536]{2,1,0:T(8,128)(2,1)S(1)}, f32[5,5,1536]{2,1,0:T(8,128)S(1)}, f32[1536]{0:T(1024)S(1)}) custom-call(s32[1,1024]{1,0:T(1,128)} %dna_hbm.1, bf16[5,5,1536]{2,1,0:T(8,128)(2,1)} %taps_hbm.1, f32[1536]{0:T(1024)} %bias_hbm.1, bf16[1536,768]{1,0:T(8,128)(2,1)} %wq_hbm.1, ...), custom_call_target="tpu_custom_call" | custom-call | flops 2000000000 | bytes 8000000 | tf_op jit(solution)/shard_map/genomic_stem/pallas_call | solution.py:441
  68.8 0.7 %write_results.1 = (bf16[1,8,768]{2,1,0:T(8,128)(2,1)}, bf16[1,8,1536]{2,1,0:T(8,128)(2,1)}, f32[5,5,1536]{2,1,0:T(8,128)}, f32[1536]{0:T(1024)}) custom-call(bf16[1,8,768]{2,1,0:T(8,128)(2,1)S(1)} %get-tuple-element.8.refs_0_, bf16[1,8,1536]{2,1,0:T(8,128)(2,1)S(1)} %get-tuple-element.9.refs_1_, f32[5,5,1536]{2,1,0:T(8,128)S(1)} %get-tuple-element.10.refs_2_, ...), custom_call_target="tpu_custom_call" | custom-call | tf_op jit(solution)/shard_map/write_results/pallas_call | solution.py:493

commit v3 on v2

--- a/solution.py
+++ b/solution.py
@@ -76,7 +76,7 @@
     dna_ref, taps_ref, bias_ref, grad_ref, weights, table, hot, hot_t, pooled_sum, slope_rows, slopes, halo,
     grad_send, grad_rows, grad_all, pool_rows, k_all, qv_all, back_send, back_rows,
     acc, chunks, near_rows, far_rows, full,
-    load_sem, halo_ss, halo_rs, g1_ss, g1_rs, g2_ss, g2_rs, p_ss, p_rs, k_ss, k_rs, q_ss, q_rs, b_ss, b_rs,
+    met_sem, load_sem, halo_ss, halo_rs, g1_ss, g1_rs, g2_ss, g2_rs, p_ss, p_rs, k_ss, k_rs, q_ss, q_rs, b_ss, b_rs,
     s_ss, s_rs,
 ):
     dp = lax.axis_index("dp")
@@ -112,28 +112,23 @@
             src_ref=src, dst_ref=dst, send_sem=ss, recv_sem=rs, device_id=device, device_id_type=MESH
         )
 
+    other_core = (dp + 1 - 2 * bits(dp, 0, 1), seq)
+    other_y = (dp + 2 - 4 * bits(dp, 1, 1), seq)
+    other_half = (dp + 16 - 32 * bits(dp, 4, 1), seq)
+    quad = bits(dp, 2, 2)
+    pairs_y = [(dp + 4 * (lax.bitwise_and(quad + step, 3) - quad), seq) for step in (1, 2, 3)]
+    column = [along_z(step) for step in range(1, DEPTH)]
+    first_met = [
+        along_seq(1), along_seq(-1), *column, *(along_x(step) for step in (4, 3, 5, 2, 6, 1, 7)),
+        other_half, *pairs_y, other_y, other_core,
+    ]
     barrier = pltpu.get_barrier_semaphore()
-
-    def greet(device):
+    for device in first_met:
         pl.semaphore_signal(barrier, inc=1, device_id=device, device_id_type=MESH)
 
-    def greet_near(step, _):
-        greet(along_near(step)[1])
-        return 0
-
-    def greet_far(step, _):
-        greet(along_far(step))
-        return 0
-
-    greet(along_seq(1))
-    greet(along_seq(-1))
-    for step in (2, 1, 3):
-        greet(along_z(step))
-    for step in range(1, RING):
-        greet(along_x(step))
-    lax.fori_loop(1, NEAR, greet_near, 0)
-    lax.fori_loop(1, FAR, greet_far, 0)
-
+    def tell(at, devices):
+        for device in devices:
+            pl.semaphore_signal(met_sem.at[at], inc=1, device_id=device, device_id_type=MESH)
 
     small = ((dna_hbm, dna_ref), (taps_hbm, taps_ref), (bias_hbm, bias_ref), (grad_hbm, grad_ref))
     reads = [pltpu.make_async_copy(hbm, ref, load_sem.at[3 + i]) for i, (hbm, ref) in enumerate(small)]
@@ -206,7 +201,7 @@
         grad_send[h] = jnp.concatenate([window[:, :128], window[:, 128:]], axis=0).astype(BF16)
 
     lax.fori_loop(0, 1, inner, 0)
-    pl.semaphore_wait(barrier, 2 + (DEPTH - 1) + (RING - 1) + (NEAR - 1) + (FAR - 1))
+    pl.semaphore_wait(barrier, len(first_met))
 
     halo_sends = [
         remote(dna_ref.at[:, SPAN - 128 : SPAN], halo.at[0], halo_ss.at[0], halo_rs.at[0], along_seq(1)),
@@ -224,6 +219,7 @@
     for copy in g1:
         copy.start()
     grad_rows[0] = grad_send[head]
+    tell(0, (other_core, other_y, other_half, *column))
 
     lax.fori_loop(1, C // LANES, inner, 0)
 
@@ -268,6 +264,8 @@
         load.wait()
     for copy in p1:
         copy.wait()
+    pl.semaphore_wait(met_sem.at[0], 6)
+    tell(1, (other_core, other_half))
     odd = bits(head, 0, 1)
     start = pl.multiple_of(384 * bits(head, 1, 1) + 128 * odd, 128)
     low = 64 * odd
@@ -402,6 +400,7 @@
     def wait_all(ref, at):
         remote(ref, ref, s_ss.at[at], s_rs.at[at], along_z(1)).wait()
 
+    pl.semaphore_wait(met_sem.at[1], 2)
     lax.fori_loop(1, NEAR, scatter, 0)
     wait_all(near_rows.at[1:NEAR], 0)
     near_sum = chunks[near].astype(F32) + jnp.sum(near_rows[1:NEAR].astype(F32), axis=0)
@@ -475,6 +474,7 @@
             pltpu.VMEM((NEAR, 16, 128), BF16),
             pltpu.VMEM((FAR, 16, 128), BF16),
             pltpu.VMEM((NEAR, 16, 128), BF16),
+            pltpu.SemaphoreType.REGULAR((2,)),
             dma((7,)), dma((2,)), dma((2,)),
             dma((DEPTH,)), dma((DEPTH,)), dma((RING,)), dma((RING,)), dma((DEPTH,)), dma((DEPTH,)),
             dma((RING,)), dma((RING,)), dma((RING,)), dma((RING,)), dma((DEPTH,)), dma((DEPTH,)),

time: 69.7 us -> 68.5 us (0.983)
  Pallas kernels: 68.9 us -> 67.7 us
    pallas_call x1, Pallas kernels: 68.2 us -> 66.9 us  [per_device(): pl.pallas_call(stem_kernel, name='genomic_stem', out_shape=(jax.ShapeDtyp...]
where the time goes in v3:
time: 68.5 us; the launch traced here: 68.3 us
  Pallas kernels  67.7 us (99%)
    pallas_call x1, Pallas kernels, per_device(): pl.pallas_call(stem_kernel, name='genomic_stem', out_shape=(jax.ShapeDtyp...  66.9 us

profile of v3, /device:TPU:1, one launch (start us, length us, event | category | flops | bytes accessed | tf_op | source)
XLA Modules:
  0.0 68.3 jit_solution(7817497966717569372)
XLA Ops:
  0.6 66.9 %genomic_stem.1 = (bf16[1,8,768]{2,1,0:T(8,128)(2,1)S(1)}, bf16[1,8,1536]{2,1,0:T(8,128)(2,1)S(1)}, f32[5,5,1536]{2,1,0:T(8,128)S(1)}, f32[1536]{0:T(1024)S(1)}) custom-call(s32[1,1024]{1,0:T(1,128)} %dna_hbm.1, bf16[5,5,1536]{2,1,0:T(8,128)(2,1)} %taps_hbm.1, f32[1536]{0:T(1024)} %bias_hbm.1, bf16[1536,768]{1,0:T(8,128)(2,1)} %wq_hbm.1, ...), custom_call_target="tpu_custom_call" | custom-call | flops 2000000000 | bytes 8000000 | tf_op jit(solution)/shard_map/genomic_stem/pallas_call | solution.py:440
  67.6 0.7 %write_results.1 = (bf16[1,8,768]{2,1,0:T(8,128)(2,1)}, bf16[1,8,1536]{2,1,0:T(8,128)(2,1)}, f32[5,5,1536]{2,1,0:T(8,128)}, f32[1536]{0:T(1024)}) custom-call(bf16[1,8,768]{2,1,0:T(8,128)(2,1)S(1)} %get-tuple-element.8.refs_0_, bf16[1,8,1536]{2,1,0:T(8,128)(2,1)S(1)} %get-tuple-element.9.refs_1_, f32[5,5,1536]{2,1,0:T(8,128)S(1)} %get-tuple-element.10.refs_2_, ...), custom_call_target="tpu_custom_call" | custom-call | tf_op jit(solution)/shard_map/write_results/pallas_call | solution.py:493

commit v4 on v3

--- a/solution.py
+++ b/solution.py
@@ -73,7 +73,7 @@
 def stem_kernel(
     dna_hbm, taps_hbm, bias_hbm, wq_hbm, wk_hbm, wv_hbm, grad_hbm,
     attended_ref, pooled_ref, conv_ref, conv_bias_ref,
-    dna_ref, taps_ref, bias_ref, grad_ref, weights, table, hot, hot_t, pooled_sum, slope_rows, slopes, halo,
+    dna_ref, taps_ref, bias_ref, grad_ref, weights, turned, table, hot, hot_t, pooled_sum, slope_rows, slopes, halo,
     grad_send, grad_rows, grad_all, pool_rows, k_all, qv_all, back_send, back_rows,
     acc, chunks, near_rows, far_rows, full,
     met_sem, load_sem, halo_ss, halo_rs, g1_ss, g1_rs, g2_ss, g2_rs, p_ss, p_rs, k_ss, k_rs, q_ss, q_rs, b_ss, b_rs,
@@ -290,7 +290,9 @@
             copy.start()
         return copies
 
-    k_all[0] = projected(1).astype(BF16)
+    key = projected(1)
+    key_tail = key[:16, 128:] + pltpu.roll(key[16:, 128:], 64, 1)
+    k_all[0] = jnp.concatenate([key[:, :128], key_tail], axis=0).astype(BF16)
     k1 = round_x(k_all, k_ss, k_rs)
     query, value = projected(0), pltpu.roll(projected(2), 64, 1)
     qv_all[0] = jnp.concatenate(
@@ -301,6 +303,13 @@
     for block in range(ROWS):
         rows = slice(block * POOL, (block + 1) * POOL)
         slopes[block] = jnp.dot(hot_t[:, rows], slope_rows[rows, :], preferred_element_type=F32)
+    def turn(part, _):
+        rows = pl.ds(pl.multiple_of(part * 128, 128), 128)
+        for i in range(3):
+            turned[i, :, rows] = weights[i, rows, :].T
+        return 0
+
+    lax.fori_loop(0, C // 128, turn, 0)
     for copy in g2:
         copy.wait()
     for copy in q1:
@@ -309,7 +318,12 @@
     everyone = RING * 32
     q = qv_all[:, :, :WIDE].reshape(everyone, WIDE)
     v = qv_all[:, :, 128:].reshape(everyone, WIDE)
-    k = k_all[...].reshape(everyone, WIDE)
+    tails = k_all[:, 32:48, :].astype(F32)
+    low_lanes = lax.broadcasted_iota(jnp.int32, tails.shape, 2) < 64
+    first_tail = jnp.where(low_lanes, tails, 0.0)
+    last_tail = jnp.where(low_lanes, pltpu.roll(tails, 64, 2), 0.0)
+    key_tail = jnp.concatenate([first_tail, last_tail], axis=1).astype(BF16)
+    k = jnp.concatenate([k_all[:, :32, :], key_tail], axis=2).reshape(everyone, WIDE)
     g = grad_all[...].reshape(everyone, WIDE)
     scale = HEAD ** (-0.5)
 
@@ -369,9 +383,9 @@
         ).astype(BF16)
 
     attended_ref[0] = joined(0)
-    d_pooled = lax.dot_general(joined(1), weights[0], NT, preferred_element_type=F32)
-    d_pooled += lax.dot_general(joined(2), weights[1], NT, preferred_element_type=F32)
-    d_pooled += lax.dot_general(joined(3), weights[2], NT, preferred_element_type=F32)
+    d_pooled = jnp.dot(joined(1), turned[0], preferred_element_type=F32)
+    d_pooled += jnp.dot(joined(2), turned[1], preferred_element_type=F32)
+    d_pooled += jnp.dot(joined(3), turned[2], preferred_element_type=F32)
     d_pooled *= 0.5 / POOL
     total = slopes[0, 0:40, :] * d_pooled[0:1]
     for block in range(1, ROWS):
@@ -383,35 +397,42 @@
             chunks[6 * tap + part] = jnp.concatenate(chunk, axis=0).astype(BF16)
     chunks[30:32] = jnp.zeros((2, 16, 128), BF16)
 
-    def scatter(step, _):
+    def outward(turn, centre):
+        side = bits(turn, 0, 1)
+        return lax.bitwise_and(centre + (1 - 2 * side) * bits(turn + 1, 1, 5), 31)
+
+    def scatter(turn, _):
+        step = outward(turn, 16)
         to, device = along_near(step)
         remote(chunks.at[to], near_rows.at[step], s_ss.at[0], s_rs.at[0], device).start()
         return 0
 
-    def spread(step, _):
+    def spread(turn, _):
+        step = outward(turn, 20)
         remote(far_rows.at[0], far_rows.at[step], s_ss.at[1], s_rs.at[1], along_far(step)).start()
         return 0
 
-    def gather(step, _):
+    def gather(turn, _):
         mine = full.at[near]
-        remote(mine, mine, s_ss.at[2], s_rs.at[2], along_near(step)[1]).start()
+        remote(mine, mine, s_ss.at[2], s_rs.at[2], along_near(outward(turn, 16))[1]).start()
         return 0
 
     def wait_all(ref, at):
         remote(ref, ref, s_ss.at[at], s_rs.at[at], along_z(1)).wait()
 
     pl.semaphore_wait(met_sem.at[1], 2)
-    lax.fori_loop(1, NEAR, scatter, 0)
+    lax.fori_loop(0, NEAR - 1, scatter, 0)
     wait_all(near_rows.at[1:NEAR], 0)
     near_sum = chunks[near].astype(F32) + jnp.sum(near_rows[1:NEAR].astype(F32), axis=0)
     far_rows[0] = near_sum.astype(BF16)
-    lax.fori_loop(1, FAR, spread, 0)
+    lax.fori_loop(0, 24, spread, 0)
+    lax.fori_loop(25, FAR, spread, 0)
     wait_all(far_rows.at[1:FAR], 1)
     far_sum = far_rows[far].astype(F32)
     for i in range(1, FAR):
         far_sum += far_rows[lax.bitwise_and(far + (FAR - i), FAR - 1)].astype(F32)
     full[near] = far_sum.astype(BF16)
-    lax.fori_loop(1, NEAR, gather, 0)
+    lax.fori_loop(0, NEAR - 1, gather, 0)
     wait_all(full.at[0 : NEAR - 1], 2)
     for tap in range(5):
         for part in range(6):
@@ -454,6 +475,7 @@
             pltpu.VMEM((C,), F32),
             pltpu.VMEM((1, ROWS, INNER), BF16),
             pltpu.VMEM((3, C, INNER), BF16),
+            pltpu.VMEM((3, INNER, C), BF16),
             pltpu.VMEM((128, C), BF16),
             pltpu.VMEM((SPAN, 128), BF16),
             pltpu.VMEM((CODES, SPAN), BF16),
@@ -465,7 +487,7 @@
             pltpu.VMEM((DEPTH, 16, 128), BF16),
             pltpu.VMEM((RING, 32, WIDE), BF16),
             pltpu.VMEM((DEPTH, 16, INNER), BF16),
-            pltpu.VMEM((RING, 32, WIDE), BF16),
+            pltpu.VMEM((RING, 48, 128), BF16),
             pltpu.VMEM((RING, 32, 384), BF16),
             pltpu.VMEM((DEPTH, 32, WIDE), BF16),
             pltpu.VMEM((DEPTH, 32, WIDE), BF16),

time: 68.5 us -> 66.9 us (0.977)
  Pallas kernels: 67.7 us -> 66.1 us
    pallas_call x1, Pallas kernels: 66.9 us -> 65.4 us  [per_device(): pl.pallas_call(stem_kernel, name='genomic_stem', out_shape=(jax.ShapeDtyp...]
where the time goes in v4:
time: 66.9 us; the launch traced here: 66.8 us
  Pallas kernels  66.1 us (99%)
    pallas_call x1, Pallas kernels, per_device(): pl.pallas_call(stem_kernel, name='genomic_stem', out_shape=(jax.ShapeDtyp...  65.4 us

profile of v4, /device:TPU:1, one launch (start us, length us, event | category | flops | bytes accessed | tf_op | source)
XLA Modules:
  0.0 66.8 jit_solution(3650396904959391960)
XLA Ops:
  0.6 65.4 %genomic_stem.1 = (bf16[1,8,768]{2,1,0:T(8,128)(2,1)S(1)}, bf16[1,8,1536]{2,1,0:T(8,128)(2,1)S(1)}, f32[5,5,1536]{2,1,0:T(8,128)S(1)}, f32[1536]{0:T(1024)S(1)}) custom-call(s32[1,1024]{1,0:T(1,128)} %dna_hbm.1, bf16[5,5,1536]{2,1,0:T(8,128)(2,1)} %taps_hbm.1, f32[1536]{0:T(1024)} %bias_hbm.1, bf16[1536,768]{1,0:T(8,128)(2,1)} %wq_hbm.1, ...), custom_call_target="tpu_custom_call" | custom-call | flops 2000000000 | bytes 8000000 | tf_op jit(solution)/shard_map/genomic_stem/pallas_call | solution.py:461
  66.0 0.7 %write_results.1 = (bf16[1,8,768]{2,1,0:T(8,128)(2,1)}, bf16[1,8,1536]{2,1,0:T(8,128)(2,1)}, f32[5,5,1536]{2,1,0:T(8,128)}, f32[1536]{0:T(1024)}) custom-call(bf16[1,8,768]{2,1,0:T(8,128)(2,1)S(1)} %get-tuple-element.8.refs_0_, bf16[1,8,1536]{2,1,0:T(8,128)(2,1)S(1)} %get-tuple-element.9.refs_1_, f32[5,5,1536]{2,1,0:T(8,128)S(1)} %get-tuple-element.10.refs_2_, ...), custom_call_target="tpu_custom_call" | custom-call | tf_op jit(solution)/shard_map/write_results/pallas_call | solution.py:515

commit v5 on v4

--- a/solution.py
+++ b/solution.py
@@ -73,10 +73,10 @@
 def stem_kernel(
     dna_hbm, taps_hbm, bias_hbm, wq_hbm, wk_hbm, wv_hbm, grad_hbm,
     attended_ref, pooled_ref, conv_ref, conv_bias_ref,
-    dna_ref, taps_ref, bias_ref, grad_ref, weights, turned, table, hot, hot_t, pooled_sum, slope_rows, slopes, halo,
+    dna_ref, taps_ref, bias_ref, grad_ref, weights, turned, table, hot, hot_t, pooled_sum, slope_rows, slopes, ends,
     grad_send, grad_rows, grad_all, pool_rows, k_all, qv_all, back_send, back_rows,
     acc, chunks, near_rows, far_rows, full,
-    met_sem, load_sem, halo_ss, halo_rs, g1_ss, g1_rs, g2_ss, g2_rs, p_ss, p_rs, k_ss, k_rs, q_ss, q_rs, b_ss, b_rs,
+    met_sem, load_sem, end_ss, end_rs, g1_ss, g1_rs, g2_ss, g2_rs, p_ss, p_rs, k_ss, k_rs, q_ss, q_rs, b_ss, b_rs,
     s_ss, s_rs,
 ):
     dp = lax.axis_index("dp")
@@ -91,8 +91,11 @@
     def along_x(step):
         return (dp, head * RING + lax.bitwise_and(col + step, RING - 1))
 
-    def along_seq(step):
-        return (dp, lax.bitwise_and(seq + (step + SEQ), SEQ - 1))
+    def beside(side, step):
+        return (
+            dp,
+            lax.bitwise_and(head + step, DEPTH - 1) * RING + lax.bitwise_and(col + (side + RING), RING - 1),
+        )
 
     def device_at(near, far):
         return (
@@ -119,7 +122,7 @@
     pairs_y = [(dp + 4 * (lax.bitwise_and(quad + step, 3) - quad), seq) for step in (1, 2, 3)]
     column = [along_z(step) for step in range(1, DEPTH)]
     first_met = [
-        along_seq(1), along_seq(-1), *column, *(along_x(step) for step in (4, 3, 5, 2, 6, 1, 7)),
+        *(beside(side, step) for side in (1, -1) for step in (2, 1, 3)), *column, *(along_x(step) for step in (4, 3, 5, 2, 6, 1, 7)),
         other_half, *pairs_y, other_y, other_core,
     ]
     barrier = pltpu.get_barrier_semaphore()
@@ -168,17 +171,18 @@
     def lanes_of(part):
         return pl.ds(pl.multiple_of(part * LANES, LANES), LANES)
 
-    def pools(blocks):
-        def body(part, _):
-            lanes = lanes_of(part)
-            for block in blocks:
-                twice, _, _ = gelu_twice(pre_act(block, lanes))
-                pooled_sum[block : block + 1, lanes] = jnp.sum(twice, axis=0, keepdims=True)
-            return 0
-
-        return body
-
-    inner, ends = pools(range(1, ROWS - 1)), pools((0, ROWS - 1))
+    row = lax.broadcasted_iota(jnp.int32, (POOL, LANES), 0)
+
+    def pools(part, _):
+        lanes = lanes_of(part)
+        for block in range(ROWS):
+            twice, _, _ = gelu_twice(pre_act(block, lanes))
+            if block == 0:
+                twice = jnp.where(row >= 2, twice, 0.0)
+            if block == ROWS - 1:
+                twice = jnp.where(row < POOL - 2, twice, 0.0)
+            pooled_sum[block : block + 1, lanes] = jnp.sum(twice, axis=0, keepdims=True)
+        return 0
 
     def slope_part(part, _):
         lanes = lanes_of(part)
@@ -200,14 +204,18 @@
             window = pltpu.roll(window, 64, 1)
         grad_send[h] = jnp.concatenate([window[:, :128], window[:, 128:]], axis=0).astype(BF16)
 
-    lax.fori_loop(0, 1, inner, 0)
+    ends[1, 0] = jnp.concatenate([codes[:, :128], codes[:, SPAN - 128 :]], axis=1)
+    lax.fori_loop(0, 1, pools, 0)
     pl.semaphore_wait(barrier, len(first_met))
 
-    halo_sends = [
-        remote(dna_ref.at[:, SPAN - 128 : SPAN], halo.at[0], halo_ss.at[0], halo_rs.at[0], along_seq(1)),
-        remote(dna_ref.at[:, 0:128], halo.at[1], halo_ss.at[1], halo_rs.at[1], along_seq(-1)),
-    ]
-    for copy in halo_sends:
+    end_sends = [
+        remote(
+            ends.at[1, 0], ends.at[1 - side, step],
+            end_ss.at[4 * (1 - side) + step], end_rs.at[4 * (1 - side) + step], beside(side, step),
+        )
+        for side, step in ((1, 2), (-1, 2), (1, 3), (-1, 3), (1, 1), (-1, 1), (1, 0), (-1, 0), (0, 2), (0, 1), (0, 3))
+    ]
+    for copy in end_sends:
         copy.start()
     g1 = [
         remote(
@@ -221,23 +229,19 @@
     grad_rows[0] = grad_send[head]
     tell(0, (other_core, other_y, other_half, *column))
 
-    lax.fori_loop(1, C // LANES, inner, 0)
-
-    for copy in halo_sends:
-        copy.wait()
-    before = jnp.where(seq == 0, -1, halo[0])
-    after = jnp.where(seq == SEQ - 1, -1, halo[1])
-    first = one_hot_rows(jnp.concatenate([before, codes[:, :256]], axis=1))
-    last = one_hot_rows(jnp.concatenate([codes[:, SPAN - 256 :], after], axis=1))
-    hot_t[:, :POOL] = first.astype(BF16)
-    hot_t[:, SPAN - POOL :] = last.astype(BF16)
-    hot[:POOL, :] = positions_first(first).astype(BF16)
-    hot[SPAN - POOL :, :] = positions_first(last).astype(BF16)
-    lax.fori_loop(0, C // LANES, ends, 0)
-
-    pooled = pooled_sum[...] * (0.5 / POOL)
-    pooled_ref[0] = pooled.astype(BF16)
-    pool_rows[0] = jnp.concatenate([pooled[:, :INNER], pooled[:, INNER:]], axis=0).astype(BF16)
+    lax.fori_loop(1, C // LANES, pools, 0)
+
+    partial = pooled_sum[...] * (0.5 / POOL)
+    rest = partial - partial.astype(BF16).astype(F32)
+    spare = [jnp.zeros((2, 256), F32)]
+    rests = [
+        jnp.concatenate([rest[at : at + 1, 256 * i : 256 * i + 256] for i in range(6)] + spare, axis=0)
+        for at in (0, ROWS - 1)
+    ]
+    pool_rows[0] = jnp.concatenate(
+        [jnp.concatenate([partial[:, :INNER], partial[:, INNER:]], axis=0), jnp.concatenate(rests, axis=0)],
+        axis=1,
+    ).astype(BF16)
     p1 = [
         remote(pool_rows.at[0], pool_rows.at[step], p_ss.at[step], p_rs.at[step], along_z(step))
         for step in range(1, DEPTH)
@@ -258,10 +262,50 @@
     for copy in g2:
         copy.start()
 
-    lax.fori_loop(0, C // LANES - 1, slope_part, 0)
+    def turn(part, _):
+        rows = pl.ds(pl.multiple_of(part * 128, 128), 128)
+        for i in range(3):
+            turned[i, :, rows] = weights[i, rows, :].T
+        return 0
 
     for load in loads:
         load.wait()
+    lax.fori_loop(0, C // 128, turn, 0)
+
+    for copy in end_sends:
+        copy.wait()
+    lane = lax.broadcasted_iota(jnp.int32, (8, 128), 1)
+    line = jnp.full((8, 128), -1, jnp.int32)
+    sides = []
+    for i in range(DEPTH):
+        level = lax.bitwise_and(head - i + DEPTH, DEPTH - 1)
+        before = jnp.where(level == 0, -1, ends[0, (i + 1) % DEPTH, :, 128:])
+        before = jnp.where(col == 0, before, ends[0, i, :, 128:])
+        after = jnp.where(level == DEPTH - 1, -1, ends[2, (i + 3) % DEPTH, :, :128])
+        after = jnp.where(col == RING - 1, after, ends[2, i, :, :128])
+        sides.append((before, after))
+        for at, move, source in (
+            (0, 2, before), (2, 2, ends[1, i, :, :128]), (8, 12, ends[1, i, :, 128:]), (12, 12, after),
+        ):
+            moved = pltpu.roll(jnp.broadcast_to(source, (8, 128)), 16 * i + move, 1)
+            line = jnp.where(lane >= 16 * i + at, moved, line)
+    line = jnp.where(lane < 16 * DEPTH, line, -1)[:1]
+    near_ends = one_hot_rows(jnp.concatenate([outside, line, outside], axis=1))
+    near_ends = positions_first(near_ends)[: 16 * DEPTH].astype(BF16)
+    twice, _, _ = gelu_twice(jnp.dot(near_ends, table[...], preferred_element_type=F32))
+    twice = twice.reshape(2 * DEPTH, 8, C)
+    place = lax.broadcasted_iota(jnp.int32, twice.shape, 1)
+    twice = jnp.where(jnp.logical_or(place == 2, place == 3), twice, 0.0)
+    end_parts = jnp.sum(twice, axis=1) * (0.5 / POOL)
+
+    before, after = sides[0]
+    first = one_hot_rows(jnp.concatenate([before, codes[:, :256]], axis=1))
+    last = one_hot_rows(jnp.concatenate([codes[:, SPAN - 256 :], after], axis=1))
+    hot_t[:, :POOL] = first.astype(BF16)
+    hot_t[:, SPAN - POOL :] = last.astype(BF16)
+    hot[:POOL, :] = positions_first(first).astype(BF16)
+    hot[SPAN - POOL :, :] = positions_first(last).astype(BF16)
+
     for copy in p1:
         copy.wait()
     pl.semaphore_wait(met_sem.at[0], 6)
@@ -271,14 +315,22 @@
     low = 64 * odd
     lane = lax.broadcasted_iota(jnp.int32, (4 * ROWS, WIDE), 1)
     keep = jnp.logical_and(lane >= low, lane < low + HEAD)
-    halves = pool_rows[...].reshape(DEPTH * 16, INNER)
+    place = lax.broadcasted_iota(jnp.int32, (ROWS, C), 0)
+    column_rows = []
+    for i in range(DEPTH):
+        sent = pool_rows[i].astype(F32)
+        wide = jnp.concatenate([sent[:8, :INNER], sent[8:, :INNER]], axis=1)
+        firsts = jnp.concatenate([sent[j : j + 1, INNER:] for j in range(6)], axis=1)
+        lasts = jnp.concatenate([sent[8 + j : 9 + j, INNER:] for j in range(6)], axis=1)
+        firsts += end_parts[2 * i : 2 * i + 1]
+        lasts += end_parts[2 * i + 1 : 2 * i + 2]
+        wide += jnp.where(place == 0, firsts, jnp.where(place == ROWS - 1, lasts, 0.0))
+        column_rows.append(wide)
+    column_rows = jnp.concatenate(column_rows, axis=0).astype(BF16)
+    pooled_ref[0] = column_rows[:ROWS]
 
     def projected(i):
-        left = jnp.dot(halves, weights[i, :INNER, pl.ds(start, WIDE)], preferred_element_type=F32)
-        right = jnp.dot(halves, weights[i, INNER:, pl.ds(start, WIDE)], preferred_element_type=F32)
-        rows = jnp.concatenate(
-            [left[16 * j : 16 * j + 8] + right[16 * j + 8 : 16 * j + 16] for j in range(DEPTH)], axis=0
-        )
+        rows = jnp.dot(column_rows, weights[i, :, pl.ds(start, WIDE)], preferred_element_type=F32)
         return pltpu.roll(jnp.where(keep, rows, 0.0), 192 * odd, 1)
 
     def round_x(ref, ss, rs):
@@ -299,17 +351,10 @@
         [query[:, :128], query[:, 128:] + value[:, :128], value[:, 128:]], axis=1
     ).astype(BF16)
     q1 = round_x(qv_all, q_ss, q_rs) + k1
-    lax.fori_loop(C // LANES - 1, C // LANES, slope_part, 0)
+    lax.fori_loop(0, C // LANES, slope_part, 0)
     for block in range(ROWS):
         rows = slice(block * POOL, (block + 1) * POOL)
         slopes[block] = jnp.dot(hot_t[:, rows], slope_rows[rows, :], preferred_element_type=F32)
-    def turn(part, _):
-        rows = pl.ds(pl.multiple_of(part * 128, 128), 128)
-        for i in range(3):
-            turned[i, :, rows] = weights[i, rows, :].T
-        return 0
-
-    lax.fori_loop(0, C // 128, turn, 0)
     for copy in g2:
         copy.wait()
     for copy in q1:
@@ -482,11 +527,11 @@
             pltpu.VMEM((ROWS, C), F32),
             pltpu.VMEM((SPAN, C), BF16),
             pltpu.VMEM((ROWS, CODES, C), F32),
-            pltpu.VMEM((2, 1, 128), jnp.int32),
+            pltpu.VMEM((3, DEPTH, 1, 256), jnp.int32),
             pltpu.VMEM((DEPTH, 16, 128), BF16),
             pltpu.VMEM((DEPTH, 16, 128), BF16),
             pltpu.VMEM((RING, 32, WIDE), BF16),
-            pltpu.VMEM((DEPTH, 16, INNER), BF16),
+            pltpu.VMEM((DEPTH, 16, INNER + 256), BF16),
             pltpu.VMEM((RING, 48, 128), BF16),
             pltpu.VMEM((RING, 32, 384), BF16),
             pltpu.VMEM((DEPTH, 32, WIDE), BF16),
@@ -497,7 +542,7 @@
             pltpu.VMEM((FAR, 16, 128), BF16),
             pltpu.VMEM((NEAR, 16, 128), BF16),
             pltpu.SemaphoreType.REGULAR((2,)),
-            dma((7,)), dma((2,)), dma((2,)),
+            dma((7,)), dma((12,)), dma((12,)),
             dma((DEPTH,)), dma((DEPTH,)), dma((RING,)), dma((RING,)), dma((DEPTH,)), dma((DEPTH,)),
             dma((RING,)), dma((RING,)), dma((RING,)), dma((RING,)), dma((DEPTH,)), dma((DEPTH,)),
             dma((3,)), dma((3,)),

time: 66.9 us -> 66.1 us (0.988)
  Pallas kernels: 66.1 us -> 65.3 us
    pallas_call x1, Pallas kernels: 65.4 us -> 64.5 us  [per_device(): pl.pallas_call(stem_kernel, name='genomic_stem', out_shape=(jax.ShapeDtyp...]
where the time goes in v5:
time: 66.1 us; the launch traced here: 65.9 us
  Pallas kernels  65.3 us (99%)
    pallas_call x1, Pallas kernels, per_device(): pl.pallas_call(stem_kernel, name='genomic_stem', out_shape=(jax.ShapeDtyp...  64.5 us

profile of v5, /device:TPU:1, one launch (start us, length us, event | category | flops | bytes accessed | tf_op | source)
XLA Modules:
  0.0 65.9 jit_solution(260887852257752582)
XLA Ops:
  0.6 64.5 %genomic_stem.1 = (bf16[1,8,768]{2,1,0:T(8,128)(2,1)S(1)}, bf16[1,8,1536]{2,1,0:T(8,128)(2,1)S(1)}, f32[5,5,1536]{2,1,0:T(8,128)S(1)}, f32[1536]{0:T(1024)S(1)}) custom-call(s32[1,1024]{1,0:T(1,128)} %dna_hbm.1, bf16[5,5,1536]{2,1,0:T(8,128)(2,1)} %taps_hbm.1, f32[1536]{0:T(1024)} %bias_hbm.1, bf16[1536,768]{1,0:T(8,128)(2,1)} %wq_hbm.1, ...), custom_call_target="tpu_custom_call" | custom-call | flops 2000000000 | bytes 8000000 | tf_op jit(solution)/shard_map/genomic_stem/pallas_call | solution.py:506
  65.2 0.7 %write_results.1 = (bf16[1,8,768]{2,1,0:T(8,128)(2,1)}, bf16[1,8,1536]{2,1,0:T(8,128)(2,1)}, f32[5,5,1536]{2,1,0:T(8,128)}, f32[1536]{0:T(1024)}) custom-call(bf16[1,8,768]{2,1,0:T(8,128)(2,1)S(1)} %get-tuple-element.8.refs_0_, bf16[1,8,1536]{2,1,0:T(8,128)(2,1)S(1)} %get-tuple-element.9.refs_1_, f32[5,5,1536]{2,1,0:T(8,128)S(1)} %get-tuple-element.10.refs_2_, ...), custom_call_target="tpu_custom_call" | custom-call | tf_op jit(solution)/shard_map/write_results/pallas_call | solution.py:560

commit v6 on v5

--- a/solution.py
+++ b/solution.py
@@ -270,7 +270,7 @@
 
     for load in loads:
         load.wait()
-    lax.fori_loop(0, C // 128, turn, 0)
+    lax.fori_loop(0, C // 128 // 2, turn, 0)
 
     for copy in end_sends:
         copy.wait()
@@ -298,14 +298,6 @@
     twice = jnp.where(jnp.logical_or(place == 2, place == 3), twice, 0.0)
     end_parts = jnp.sum(twice, axis=1) * (0.5 / POOL)
 
-    before, after = sides[0]
-    first = one_hot_rows(jnp.concatenate([before, codes[:, :256]], axis=1))
-    last = one_hot_rows(jnp.concatenate([codes[:, SPAN - 256 :], after], axis=1))
-    hot_t[:, :POOL] = first.astype(BF16)
-    hot_t[:, SPAN - POOL :] = last.astype(BF16)
-    hot[:POOL, :] = positions_first(first).astype(BF16)
-    hot[SPAN - POOL :, :] = positions_first(last).astype(BF16)
-
     for copy in p1:
         copy.wait()
     pl.semaphore_wait(met_sem.at[0], 6)
@@ -351,10 +343,18 @@
         [query[:, :128], query[:, 128:] + value[:, :128], value[:, 128:]], axis=1
     ).astype(BF16)
     q1 = round_x(qv_all, q_ss, q_rs) + k1
+    before, after = sides[0]
+    first = one_hot_rows(jnp.concatenate([before, codes[:, :256]], axis=1))
+    last = one_hot_rows(jnp.concatenate([codes[:, SPAN - 256 :], after], axis=1))
+    hot_t[:, :POOL] = first.astype(BF16)
+    hot_t[:, SPAN - POOL :] = last.astype(BF16)
+    hot[:POOL, :] = positions_first(first).astype(BF16)
+    hot[SPAN - POOL :, :] = positions_first(last).astype(BF16)
     lax.fori_loop(0, C // LANES, slope_part, 0)
     for block in range(ROWS):
         rows = slice(block * POOL, (block + 1) * POOL)
         slopes[block] = jnp.dot(hot_t[:, rows], slope_rows[rows, :], preferred_element_type=F32)
+    lax.fori_loop(C // 128 // 2, C // 128, turn, 0)
     for copy in g2:
         copy.wait()
     for copy in q1:

time: 66.1 us -> 65.8 us (level)
  no operation moved by 1% of the time
where the time goes in v6:
time: 65.8 us; the launch traced here: 65.7 us
  Pallas kernels  65.1 us (99%)
    pallas_call x1, Pallas kernels, per_device(): pl.pallas_call(stem_kernel, name='genomic_stem', out_shape=(jax.ShapeDtyp...  64.3 us

profile of v6, /device:TPU:1, one launch (start us, length us, event | category | flops | bytes accessed | tf_op | source)
XLA Modules:
  0.0 65.7 jit_solution(824007424502399800)
XLA Ops:
  0.6 64.3 %genomic_stem.1 = (bf16[1,8,768]{2,1,0:T(8,128)(2,1)S(1)}, bf16[1,8,1536]{2,1,0:T(8,128)(2,1)S(1)}, f32[5,5,1536]{2,1,0:T(8,128)S(1)}, f32[1536]{0:T(1024)S(1)}) custom-call(s32[1,1024]{1,0:T(1,128)} %dna_hbm.1, bf16[5,5,1536]{2,1,0:T(8,128)(2,1)} %taps_hbm.1, f32[1536]{0:T(1024)} %bias_hbm.1, bf16[1536,768]{1,0:T(8,128)(2,1)} %wq_hbm.1, ...), custom_call_target="tpu_custom_call" | custom-call | flops 2000000000 | bytes 8000000 | tf_op jit(solution)/shard_map/genomic_stem/pallas_call | solution.py:506
  65.0 0.7 %write_results.1 = (bf16[1,8,768]{2,1,0:T(8,128)(2,1)}, bf16[1,8,1536]{2,1,0:T(8,128)(2,1)}, f32[5,5,1536]{2,1,0:T(8,128)}, f32[1536]{0:T(1024)}) custom-call(bf16[1,8,768]{2,1,0:T(8,128)(2,1)S(1)} %get-tuple-element.8.refs_0_, bf16[1,8,1536]{2,1,0:T(8,128)(2,1)S(1)} %get-tuple-element.9.refs_1_, f32[5,5,1536]{2,1,0:T(8,128)S(1)} %get-tuple-element.10.refs_2_, ...), custom_call_target="tpu_custom_call" | custom-call | tf_op jit(solution)/shard_map/write_results/pallas_call | solution.py:560

commit v7 on v6

--- a/solution.py
+++ b/solution.py
@@ -428,9 +428,8 @@
         ).astype(BF16)
 
     attended_ref[0] = joined(0)
-    d_pooled = jnp.dot(joined(1), turned[0], preferred_element_type=F32)
-    d_pooled += jnp.dot(joined(2), turned[1], preferred_element_type=F32)
-    d_pooled += jnp.dot(joined(3), turned[2], preferred_element_type=F32)
+    d_rows = jnp.concatenate([joined(1), joined(2), joined(3)], axis=1)
+    d_pooled = jnp.dot(d_rows, turned[...].reshape(3 * INNER, C), preferred_element_type=F32)
     d_pooled *= 0.5 / POOL
     total = slopes[0, 0:40, :] * d_pooled[0:1]
     for block in range(1, ROWS):

time: 65.8 us -> 65.9 us (level)
  no operation moved by 1% of the time
where the time goes in v7:
time: 65.9 us; the launch traced here: 65.7 us
  Pallas kernels  65.1 us (99%)
    pallas_call x1, Pallas kernels, per_device(): pl.pallas_call(stem_kernel, name='genomic_stem', out_shape=(jax.ShapeDtyp...  64.3 us

profile of v7, /device:TPU:1, one launch (start us, length us, event | category | flops | bytes accessed | tf_op | source)
XLA Modules:
  0.0 65.7 jit_solution(5114728211942106275)
XLA Ops:
  0.6 64.3 %genomic_stem.1 = (bf16[1,8,768]{2,1,0:T(8,128)(2,1)S(1)}, bf16[1,8,1536]{2,1,0:T(8,128)(2,1)S(1)}, f32[5,5,1536]{2,1,0:T(8,128)S(1)}, f32[1536]{0:T(1024)S(1)}) custom-call(s32[1,1024]{1,0:T(1,128)} %dna_hbm.1, bf16[5,5,1536]{2,1,0:T(8,128)(2,1)} %taps_hbm.1, f32[1536]{0:T(1024)} %bias_hbm.1, bf16[1536,768]{1,0:T(8,128)(2,1)} %wq_hbm.1, ...), custom_call_target="tpu_custom_call" | custom-call | flops 2000000000 | bytes 8000000 | tf_op jit(solution)/shard_map/genomic_stem/pallas_call | solution.py:505
  65.0 0.7 %write_results.1 = (bf16[1,8,768]{2,1,0:T(8,128)(2,1)}, bf16[1,8,1536]{2,1,0:T(8,128)(2,1)}, f32[5,5,1536]{2,1,0:T(8,128)}, f32[1536]{0:T(1024)}) custom-call(bf16[1,8,768]{2,1,0:T(8,128)(2,1)S(1)} %get-tuple-element.8.refs_0_, bf16[1,8,1536]{2,1,0:T(8,128)(2,1)S(1)} %get-tuple-element.9.refs_1_, f32[5,5,1536]{2,1,0:T(8,128)S(1)} %get-tuple-element.10.refs_2_, ...), custom_call_target="tpu_custom_call" | custom-call | tf_op jit(solution)/shard_map/write_results/pallas_call | solution.py:559
